TPU v7x, 512 devices: a whole 4x8x8 slice. The times are simulated.
512 devices in a mesh: tm: 64 (over x, z, core), region: 8 (over y).
Axes of the slice: x: 4, y: 8, z: 8, core: 2. Of those that a mesh axis runs over, the one named last changes fastest.
Arguments:
- activity: bfloat16 [6144, 131072], P('region', 'tm'), may hold values from -6 to 6
- test_matrix: bfloat16 [131072, 512], P('tm', 'region'), may hold values from -0.015625 to 0.015625
- basis_mix: float32 [512, 64], replicated, may hold values from -0.25 to 0.25
- recurrent: float32 [64, 64], replicated, may hold values from -0.75 to 0.75
- latent_bias: float32 [64], replicated, may hold values from -2 to 2
- readout: bfloat16 [6144, 64], P('region'), may hold values from -0.75 to 0.75
- region_in: bfloat16 [6144, 8], P('region'), may hold values from -0.21875 to 0.21875
- region_out: bfloat16 [6144, 8], P('region'), may hold values from -1 to 1
- region_of_block: int32 [48], replicated, may hold values from 0 to 7, never falling along the last dimension, each value on 1 to 12 neighbouring positions
- region_mask: int32 [8, 8], replicated, may hold values 0 or 1
Outputs:
- latents: float32 [64, 131072], P(None, 'tm')
- frame_loss: float32 [131072], P('tm')
- readout_score: float32 [6144, 64], P('region')
Inputs may be any that keep to these rules, and one draw needn't show every extreme that they name: `region_of_block`: blocks of one region are consecutive, every region holds at least one block, and no region holds more than 12 blocks.
All inputs are finite; a program needn't handle non-finite values.
Results may differ from a plain program's by a relative error of at most 0.0028.
Values may be sent and summed in bfloat16 or wider, within the bound.
No kernel may reach another device: no remote copies, remote signals or barrier semaphores. Data moves between devices by JAX's collectives and lax.ppermute only.
A program may use at most 64 MiB of HBM per device.

v0:
```python
import jax
import jax.numpy as jnp
from jax import lax
from jax.sharding import PartitionSpec as P

BLOCK = 128


precise = lax.Precision.HIGHEST
epsilon = 1e-05


def from_behind(block, axis, distance):
    devices = range(lax.axis_size(axis))
    route = [(i - distance, i) for i in devices if i - distance in devices]
    return lax.ppermute(block, axis, route)


def orthonormal(sketch, gram):
    lower = jnp.linalg.cholesky(gram)
    return jax.scipy.linalg.solve_triangular(lower, sketch.T, lower=True).T


def region_tables(block_regions, region_mask, region_in, region_out):
    regions = region_mask.shape[0]
    signal_width = region_in.shape[1]
    block_total = block_regions.shape[0]
    block_rows = region_in.shape[0] // block_total
    onehot = (block_regions[:, None] == jnp.arange(regions, dtype=jnp.int32)[None, :]).astype(
        jnp.float32
    )
    onehot = jnp.broadcast_to(onehot[:, None, :], (block_total, block_rows, regions)).reshape(
        block_total * block_rows, regions
    )
    allowed = jnp.dot(onehot, region_mask.astype(jnp.float32), precision=precise)
    region_feed = (onehot[:, :, None] * region_in.astype(jnp.float32)[:, None, :]).reshape(
        -1, regions * signal_width
    )
    spread = (allowed[:, :, None] * region_out.astype(jnp.float32)[:, None, :]).reshape(
        -1, regions * signal_width
    )
    return (region_feed.astype(jnp.bfloat16), spread.astype(jnp.bfloat16))


def local(
    activity,
    test_matrix,
    basis_mix,
    recurrent,
    latent_bias,
    readout,
    region_in,
    region_out,
    region_of_block,
    region_mask,
):
    neurons_here, frames_here = activity.shape
    contract = (((0,), (0,)), ((), ()))
    block_count = neurons_here // BLOCK
    my_blocks = lax.dynamic_slice_in_dim(
        region_of_block, lax.axis_index("region") * block_count, block_count
    )
    region_feed, spread = region_tables(my_blocks, region_mask, region_in, region_out)
    test_full = lax.all_gather(test_matrix, "region", axis=1, tiled=True)
    sketch_rows = lax.psum_scatter(
        jnp.dot(activity, test_full, preferred_element_type=jnp.float32),
        "tm",
        scatter_dimension=0,
        tiled=True,
    )
    gram = lax.psum(jnp.dot(sketch_rows.T, sketch_rows, precision=precise), ("tm", "region"))
    loading_rows = jnp.dot(orthonormal(sketch_rows, gram), basis_mix, precision=precise).astype(
        jnp.bfloat16
    )
    latent_part = lax.dot_general(
        lax.all_gather(loading_rows, "tm", axis=0, tiled=True),
        activity,
        contract,
        preferred_element_type=jnp.float32,
    )
    signal_part = lax.dot_general(
        region_feed, activity, contract, preferred_element_type=jnp.float32
    )
    latents, signals = lax.psum((latent_part, signal_part), "region")
    prior_latent, prior_signal = from_behind((latents[:, -1:], signals[:, -1:]), "tm", 1)
    lagged_latents = jnp.concatenate([prior_latent, latents[:, :-1]], axis=1)
    lagged_signals = jnp.concatenate([prior_signal, signals[:, :-1]], axis=1)
    hidden = jnp.tanh(jnp.dot(recurrent, lagged_latents, precision=precise) + latent_bias[:, None])
    predicted = jnp.dot(readout, hidden.astype(jnp.bfloat16), preferred_element_type=jnp.float32)
    predicted = predicted + jnp.dot(
        spread, lagged_signals.astype(jnp.bfloat16), preferred_element_type=jnp.float32
    )
    error = activity.astype(jnp.float32) - predicted
    squared = error * error
    cross, error_sq, hidden_sq = lax.psum(
        (
            jnp.dot(error, hidden.T, precision=precise),
            jnp.sum(squared, axis=1),
            jnp.sum(hidden * hidden, axis=1),
        ),
        "tm",
    )
    frame_sq = lax.psum(jnp.sum(squared, axis=0), "region")
    frames_all = frames_here * lax.axis_size("tm")
    frame_loss = frame_sq / (neurons_here * lax.axis_size("region"))
    readout_score = cross / jnp.sqrt(
        frames_all
        * (error_sq[:, None] / frames_all + epsilon)
        * (hidden_sq[None, :] / frames_all + epsilon)
    )
    return (latents, frame_loss, readout_score)


def solution(mesh):
    in_specs = (
        P("region", "tm"),
        P("tm", "region"),
        P(),
        P(),
        P(),
        P("region", None),
        P("region", None),
        P("region", None),
        P(),
        P(),
    )
    out_specs = (P(None, "tm"), P("tm"), P("region", None))
    return jax.shard_map(local, mesh=mesh, in_specs=in_specs, out_specs=out_specs, check_vma=False)
```

profile of v0, /device:TPU:6, one launch (start us, length us, event | category | flops | bytes accessed | tf_op | source)
XLA Modules:
  0.0 1048.3 jit_solution(13345600834286897948)
XLA Ops:
  8.0 50.3 %all-gather.3.cloned.1.call-done = bf16[2048,512]{0,1:T(8,128)(2,1)} async-done(((bf16[2048,64]{0,1:T(8,128)(2,1)}), bf16[2048,512]{0,1:T(8,128)(2,1)}) %all-gather.3.cloned.1.call-update) | async-done | bytes 2097168 | tf_op jit(solution)/shard_map/all_gather | solution.py:64
  58.3 5.5 fusion.73
  63.8 119.6 %fusion = f32[16,512]{1,0:T(8,128)S(1)} fusion(f32[768,512]{1,0:T(8,128)} %fusion.73), kind=kCustom, calls=%all-reduce-scatter | all-reduce-scatter fusion | flops 524289 | bytes 1607680
  184.7 20.9 %collective-permute-start.16 = (f32[16,512]{1,0:T(8,128)S(1)}, f32[16,512]{1,0:T(8,128)S(1)}, u32[]{:S(2)}, u32[]{:S(2)}) collective-permute-start(f32[16,512]{1,0:T(8,128)S(1)} %fusion), channel_id=1, source_target_pairs={{0,120},{8,128},{16,136},{24,144},{32,152},{40,160},{48,168},{56,1... | collective-permute-start | bytes 98312
  240.3 23.2 %concatenate.21 = f32[268,512]{1,0:T(8,128)} concatenate(f32[12,512]{1,0:T(8,128)S(1)} %collective-permute-done.17, f32[16,512]{1,0:T(8,128)S(1)} %collective-permute-done.16, f32[16,512]{1,0:T(8,128)S(1)} %collective-permute-done.15, f32[16,512]{1,0:T(8,128)S(1)} %collective-permute-done.14, f32[16,512]{1,0:T(8,128)S(1)} %collective-permute-done.13, ...), dimensions={0} | concatenate | bytes 1097728
  269.6 275.9 %all-reduce.9.cloned.1.call-done = f32[512,512]{0,1:T(8,128)} async-done(((f32[512,512]{0,1:T(8,128)}), f32[512,512]{0,1:T(8,128)}) %all-reduce.9.cloned.1.call-update) | async-done | bytes 1048592 | tf_op jit(solution)/shard_map/psum | solution.py:71
  550.8 11.7 %cholesky.104 = f32[128,128]{1,0:T(8,128)S(1)} custom-call(f32[128,128]{1,0:T(8,128)S(1)} %cholesky.266), custom_call_target="Cholesky" | custom-call | tf_op jit(solution)/shard_map/jit(cholesky)/cholesky | solution.py:20
  562.5 9.8 custom-call.31
  577.3 12.5 %cholesky.217 = f32[128,128]{1,0:T(8,128)S(1)} custom-call(f32[128,128]{1,0:T(8,128)} %cholesky.270), custom_call_target="Cholesky" | custom-call | tf_op jit(solution)/shard_map/jit(cholesky)/cholesky | solution.py:20
  590.5 10.8 %custom-call.32 = f32[1,128,128]{1,2,0:T(8,128)S(1)} custom-call(f32[1,128,128]{2,1,0:T(8,128)} %get-tuple-element.31), custom_call_target="InvertDiagBlocksLowerTriangular" | custom-call | tf_op jit(solution)/shard_map/jit(cholesky)/cholesky | solution.py:20
  603.7 11.7 %cholesky.238 = f32[128,128]{1,0:T(8,128)S(1)} custom-call(f32[128,128]{1,0:T(8,128)S(1)} %cholesky.275), custom_call_target="Cholesky" | custom-call | tf_op jit(solution)/shard_map/jit(cholesky)/cholesky | solution.py:20
  616.7 9.8 custom-call.33
  628.8 12.1 %cholesky.255 = f32[128,128]{1,0:T(8,128)S(1)} custom-call(f32[128,128]{1,0:T(8,128)S(1)} %convolution_subtract_fusion.2), custom_call_target="Cholesky" | custom-call | tf_op jit(solution)/shard_map/jit(cholesky)/cholesky | solution.py:20
  647.7 14.4 %while.1 = (s32[]{:T(128)}, f32[512,512]{1,0:T(8,128)}, s32[4,2]{0,1:T(2,128)S(1)}, f32[4,128,128]{2,1,0:T(8,128)}, s32[]{:T(128)}) while((s32[]{:T(128)}, f32[512,512]{1,0:T(8,128)}, s32[4,2]{0,1:T(2,128)S(1)}, f32[4,128,128]{2,1,0:T(8,128)}, s32[]{:T(128)}) %tuple.34), condition=%wide.while_cond, body=%wide.while_body.sunk | while | flops 2 | bytes 132205 | solution.py:21
  648.4 3.0 bitcast_dynamic-update-slice_fusion.2
  652.0 3.0 bitcast_dynamic-update-slice_fusion.2
  662.2 40.1 %custom-call.34 = f32[4,128,128]{1,2,0:T(8,128)S(1)} custom-call(f32[4,128,128]{2,1,0:T(8,128)} %get-tuple-element.10), custom_call_target="InvertDiagBlocksLowerTriangular" | custom-call | tf_op jit(solution)/shard_map/jit(_solve_triangular)/triangular_solve | solution.py:21
  709.4 43.4 %all-gather = bf16[64,12,64]{2,1,0:T(8,128)(2,1)S(1)} all-gather(bf16[1,12,64]{2,1,0:T(8,128)(2,1)S(1)} %fusion.3), channel_id=1, replica_groups=mesh['tm'=64,'region'=8] {'tm'}, dimensions={0}, use_global_device_ids=true | all-gather | bytes 99840 | tf_op jit(solution)/shard_map/all_gather | solution.py:76
  756.1 37.7 %all-reduce.14 = bf16[64,2048]{1,0:T(8,128)(2,1)S(1)} all-reduce(f32[64,2048]{1,0:T(8,128)} %fusion.26), channel_id=1, replica_groups=mesh['tm'=64,'region'=8] {'region'}, use_global_device_ids=true, to_apply=%region_11.12 | all-reduce | flops 131072 | bytes 786432 | tf_op jit(solution)/shard_map/psum | solution.py:84
  796.4 35.3 %all-reduce.11.cloned.1.call-done = f32[64,2048]{1,0:T(8,128)} async-done(((f32[64,2048]{1,0:T(8,128)}), f32[64,2048]{1,0:T(8,128)}) %all-reduce.11.cloned.1.call-update) | async-done | bytes 524304 | tf_op jit(solution)/shard_map/psum | solution.py:84
  847.4 4.8 fusion.75
  852.2 108.7 %all-reduce.3 = (f32[64]{0:T(128)S(1)}, f32[768]{0:T(1024)S(1)}) all-reduce(f32[64]{0:T(128)S(1)} %get-tuple-element.38, f32[768]{0:T(1024)S(1)} %get-tuple-element.11), channel_id=1, replica_groups=mesh['tm'=64,'region'=8] {'tm'}, use_global_device_ids=true, to_apply=%region_18.19 | all-reduce | flops 832 | bytes 6656 | tf_op jit(solution)/shard_map/psum | solution.py:95
  960.9 16.7 %psum.52 = f32[2048]{0:T(1024)S(1)} all-reduce(f32[2048]{0:T(1024)S(1)} %get-tuple-element.12), channel_id=1, replica_groups=mesh['tm'=64,'region'=8] {'region'}, use_global_device_ids=true, to_apply=%region_13.14 | all-reduce | flops 2048 | bytes 16384 | tf_op jit(solution)/shard_map/psum | solution.py:103
  978.2 60.9 %all-reduce.13.cloned.1.call-done = f32[768,64]{0,1:T(8,128)} async-done(((f32[768,64]{0,1:T(8,128)}), f32[768,64]{0,1:T(8,128)}) %all-reduce.13.cloned.1.call-update) | async-done | bytes 196624 | tf_op jit(solution)/shard_map/psum | solution.py:95
  (142 shorter events, 103.3 us)
Async XLA Ops:
  7.2 702.1 %copy-start = (f32[512,64]{0,1:T(8,128)S(1)}, f32[512,64]{0,1:T(8,128)}, u32[]{:S(2)}) copy-start(f32[512,64]{0,1:T(8,128)} %param.12) | copy-start | bytes 393220
  7.2 51.1 %all-gather.3.cloned.1.call-start = ((), (), s32[]{:S(2)}) async-start(), calls=%async_computation | async-start | bytes 2359296 | tf_op jit(solution)/shard_map/all_gather | solution.py:64
  7.9 205.4 %copy-start.16 = (s32[48]{0:T(128)S(1)}, s32[48]{0:T(128)}, u32[]{:S(2)}) copy-start(s32[48]{0:T(128)} %param.18) | copy-start | bytes 580
  7.9 537.5 %all-reduce.9.cloned.1.call-start = ((), (), s32[]{:S(2)}) async-start(), calls=%async_computation.1 | async-start | bytes 2097152 | tf_op jit(solution)/shard_map/psum | solution.py:71
  183.4 28.0 %collective-permute-start.17 = (f32[12,512]{1,0:T(8,128)S(1)}, f32[12,512]{1,0:T(8,128)S(1)}, u32[]{:S(2)}, u32[]{:S(2)}) collective-permute-start(f32[12,512]{1,0:T(8,128)S(1)} %slice.146), channel_id=1, source_target_pairs={{0,128},{8,136},{16,144},{24,152},{32,160},{40,168},{48,176},{56,1... | collective-permute-start | bytes 73736
  184.7 28.7 %collective-permute-start.16 = (f32[16,512]{1,0:T(8,128)S(1)}, f32[16,512]{1,0:T(8,128)S(1)}, u32[]{:S(2)}, u32[]{:S(2)}) collective-permute-start(f32[16,512]{1,0:T(8,128)S(1)} %fusion), channel_id=1, source_target_pairs={{0,120},{8,128},{16,136},{24,144},{32,152},{40,160},{48,168},{56,1... | collective-permute-start | bytes 98312
  205.5 9.7 collective-permute-start.15
  207.5 9.8 collective-permute-start.14
  209.4 9.8 collective-permute-start.13
  211.3 9.8 collective-permute-start.12
  213.4 9.8 collective-permute-start.11
  215.3 10.2 collective-permute-start.10
  217.2 10.8 %collective-permute-start.9 = (f32[16,512]{1,0:T(8,128)S(1)}, f32[16,512]{1,0:T(8,128)S(1)}, u32[]{:S(2)}, u32[]{:S(2)}) collective-permute-start(f32[16,512]{1,0:T(8,128)S(1)} %fusion), channel_id=1, source_target_pairs={{0,64},{8,72},{16,80},{24,88},{32,96},{40,104},{48,112},{56,120},{... | collective-permute-start | bytes 98312
  219.2 10.7 %collective-permute-start.8 = (f32[16,512]{1,0:T(8,128)S(1)}, f32[16,512]{1,0:T(8,128)S(1)}, u32[]{:S(2)}, u32[]{:S(2)}) collective-permute-start(f32[16,512]{1,0:T(8,128)S(1)} %fusion), channel_id=1, source_target_pairs={{0,56},{8,64},{16,72},{24,80},{32,88},{40,96},{48,104},{56,112},{6... | collective-permute-start | bytes 98312
  221.1 11.8 %collective-permute-start.7 = (f32[16,512]{1,0:T(8,128)S(1)}, f32[16,512]{1,0:T(8,128)S(1)}, u32[]{:S(2)}, u32[]{:S(2)}) collective-permute-start(f32[16,512]{1,0:T(8,128)S(1)} %fusion), channel_id=1, source_target_pairs={{0,48},{8,56},{16,64},{24,72},{32,80},{40,88},{48,96},{56,104},{64... | collective-permute-start | bytes 98312
  223.1 14.6 %collective-permute-start.6 = (f32[16,512]{1,0:T(8,128)S(1)}, f32[16,512]{1,0:T(8,128)}, u32[]{:S(2)}, u32[]{:S(2)}) collective-permute-start(f32[16,512]{1,0:T(8,128)S(1)} %fusion), channel_id=1, source_target_pairs={{0,40},{8,48},{16,56},{24,64},{32,72},{40,80},{48,88},{56,96},{64,... | collective-permute-start | bytes 98312
  225.5 12.2 %collective-permute-start.5 = (f32[16,512]{1,0:T(8,128)S(1)}, f32[16,512]{1,0:T(8,128)}, u32[]{:S(2)}, u32[]{:S(2)}) collective-permute-start(f32[16,512]{1,0:T(8,128)S(1)} %fusion), channel_id=1, source_target_pairs={{0,32},{8,40},{16,48},{24,56},{32,64},{40,72},{48,80},{56,88},{64,... | collective-permute-start | bytes 98312
  228.0 9.8 collective-permute-start.4
  229.9 8.2 collective-permute-start.3
  232.9 7.4 collective-permute-start.2
  266.4 565.2 %all-reduce.11.cloned.1.call-start = ((), (), s32[]{:S(2)}) async-start(), calls=%async_computation.2 | async-start | bytes 1048576 | tf_op jit(solution)/shard_map/psum | solution.py:84
  756.0 283.1 %all-reduce.13.cloned.1.call-start = ((), (), s32[]{:S(2)}) async-start(), calls=%async_computation.3 | async-start | bytes 393216 | tf_op jit(solution)/shard_map/psum | solution.py:95
  794.4 50.4 %collective-permute-start.1 = (bf16[64,1]{1,0:T(8,128)(2,1)}, bf16[64,1]{1,0:T(8,128)(2,1)}, u32[]{:S(2)}, u32[]{:S(2)}) collective-permute-start(bf16[64,1]{1,0:T(8,128)(2,1)} %slice.144), channel_id=1, source_target_pairs={{0,8},{8,16},{16,24},{24,32},{32,40},{40,48},{48,56},{56,64},{64,7... | collective-permute-start | bytes 392 | tf_op jit(solution)/shard_map/ppermute | solution.py:16
  833.1 7.6 collective-permute-start
  (15 other events, 708.4 us)
Sparse Core Ops, SparseCore 0:
  10.1 48.1 all-gather.2
  266.6 278.8 all-reduce.8
  756.1 75.4 all-reduce.10
  852.3 186.7 all-reduce.12
where the time goes:
time: 1060 us; the launch traced here: 1050 us
  waiting for transfers between devices  428 us (40%)
  blocking collectives  326 us (31%)
  other arithmetic  130 us (12%)
  starting transfers between devices  55 us (5%)
  local copies, waits for them, and re-layouts  52.3 us (5%)
  matrix products  39.4 us (4%)
  between operations  17.7 us (2%)
    psum x1, waiting for transfers between devices, local(): lax.psum(jnp.dot(sketch_rows.T, sketch_rows, precision=precise), ('tm', '...  276 us
    unnamed x1, blocking collectives  120 us
    psum x1, blocking collectives, local(): lax.psum((jnp.dot(error, hidden.T, precision=precise), jnp.sum(squared, a...  109 us
    another operation x14, other arithmetic, orthonormal(): lower = jnp.linalg.cholesky(gram)  82.5 us
    psum x1, waiting for transfers between devices, local(): lax.psum((jnp.dot(error, hidden.T, precision=precise), jnp.sum(squared, a...  60.9 us
    unnamed x16, starting transfers between devices  50.7 us
    all_gather x1, waiting for transfers between devices, local(): test_full = lax.all_gather(test_matrix, 'region', axis=1, tiled=True)  50.3 us
    all_gather x1, blocking collectives, local(): lax.all_gather(loading_rows, 'tm', axis=0, tiled=True)  43.4 us
  transfers between devices with their start and end apart: 22, of which 8 were waited for; matrix products, arithmetic and copies ran while one was open for 1% of the time, Pallas kernels for 0%

commit v1 on v0

v1 whole, which is shorter than its diff:
```python
import functools

import jax
import jax.numpy as jnp
from jax import lax
from jax.experimental import pallas as pl
from jax.experimental.pallas import tpu as pltpu
from jax.sharding import Mesh
from jax.sharding import PartitionSpec as P

BLOCK = 128
CORES = 2
SLAB = ("chip", "core")

precise = lax.Precision.HIGHEST
epsilon = 1e-05
full = jnp.float32
half = jnp.bfloat16


def product(a, b, ca, cb, precision=None):
    return lax.dot_general(
        a, b, (((ca,), (cb,)), ((), ())), precision=precision, preferred_element_type=full
    )


def other_core(x):
    return lax.ppermute(x, "core", [(0, 1), (1, 0)])


def scatter_sum(pieces, axis):
    return jnp.sum(lax.all_to_all(pieces, axis, 0, 0), axis=0)


def share(x, axis):
    copies = jnp.broadcast_to(x[None], (lax.axis_size(axis),) + x.shape)
    return lax.all_to_all(lax.optimization_barrier(copies), axis, 0, 0)


def in_core_order(mine, theirs):
    first = lax.axis_index("core") == 0
    return jnp.where(first, mine, theirs), jnp.where(first, theirs, mine)


def inverse_factor(tile):
    n = tile.shape[0]
    groups = n // 8
    sub = lax.broadcasted_iota(jnp.int32, (8, n), 0)
    lane = lax.broadcasted_iota(jnp.int32, (8, n), 1)

    def column(x, j):
        return jnp.broadcast_to(x[:, j : j + 1], x.shape)

    def row(x, j):
        return jnp.broadcast_to(x[j : j + 1, :], x.shape)

    left = [tile[8 * q : 8 * q + 8, :] for q in range(groups)]
    right = [jnp.where(lane == sub + 8 * q, full(1), full(0)) for q in range(groups)]
    for p in range(groups):
        at = [column(left[p], 8 * p + j) for j in range(8)]
        lp, rp = left[p], right[p]
        pivots = jnp.ones_like(lp)
        inverse, left_rows, right_rows, pivot_rows = [], [], [], []
        for j in range(8):
            pivot = row(at[j], j)
            pivots = jnp.where(sub == j, pivot, pivots)
            inverse.append(1.0 / pivot)
            left_rows.append(row(lp, j))
            right_rows.append(row(rp, j))
            pivot_rows.append([row(at[k], j) for k in range(j + 1, 8)])
            if j < 7:
                factor = jnp.where(sub > j, at[j] * inverse[j], 0.0)
                for k in range(j + 1, 8):
                    at[k] = at[k] - factor * pivot_rows[j][k - j - 1]
                lp = lp - factor * left_rows[j]
                rp = rp - factor * right_rows[j]
        right[p] = rp * lax.rsqrt(pivots)
        for q in range(p + 1, groups):
            at = [column(left[q], 8 * p + j) for j in range(8)]
            lq, rq = left[q], right[q]
            for j in range(8):
                factor = at[j] * inverse[j]
                for k in range(j + 1, 8):
                    at[k] = at[k] - factor * pivot_rows[j][k - j - 1]
                lq = lq - factor * left_rows[j]
                rq = rq - factor * right_rows[j]
            left[q], right[q] = lq, rq
    return jnp.concatenate(right, axis=0)


def latents_kernel(
    gram_low, gram_high, sketch_low, sketch_high, mix, before, activity, out, work, inverse, weights
):
    n = work.shape[0]
    mid = n // 2
    work[:mid, :] = gram_low[...]
    work[mid:, :] = gram_high[...]
    starts = range(0, n, BLOCK)
    for a in starts:
        e = a + BLOCK
        inverse[a:e, :] = inverse_factor(work[a:e, a:e])
        if e < n:
            below = product(work[e:, a:e], inverse[a:e, :], 1, 1, precise)
            work[e:, a:e] = below
            work[e:, e:] = work[e:, e:] - product(below, below, 1, 1, precise)
    for a in reversed(starts):
        e = a + BLOCK
        rest = mix[:, a:e]
        if e < n:
            rest = rest - product(weights[:, e:], work[e:, a:e], 1, 0, precise)
        weights[:, a:e] = product(rest, inverse[a:e, :], 1, 0, precise)
    loading = product(weights[:, :mid], sketch_low[...], 1, 0, precise)
    loading = loading + product(weights[:, mid:], sketch_high[...], 1, 0, precise)
    loading = loading.astype(half)
    rank = loading.shape[0]
    pieces, rows, width = out.shape
    prior = product(before[...], loading, 1, 1)
    for i in range(pieces):
        out[i, :rank, :] = product(
            loading, activity[:, i * width : (i + 1) * width], 1, 0
        )
        out[i, rank:, :] = jnp.zeros((rows - rank, width), full)
        out[i, rank:, :rank] = prior[: rows - rank, :]


def in_vmem(count):
    return [pl.BlockSpec(memory_space=pltpu.VMEM)] * count


def latent_parts(gram, sketch, mix, before, activity, pieces):
    n = mix.shape[1]
    rank = mix.shape[0]
    frames = activity.shape[1]
    return pl.pallas_call(
        latents_kernel,
        out_shape=jax.ShapeDtypeStruct((pieces, rank + 8, frames // pieces), full),
        in_specs=in_vmem(7),
        out_specs=in_vmem(1)[0],
        scratch_shapes=[
            pltpu.VMEM((n, n), full),
            pltpu.VMEM((n, BLOCK), full),
            pltpu.VMEM((rank, n), full),
        ],
        compiler_params=pltpu.CompilerParams(vmem_limit_bytes=40 * 2**20),
        cost_estimate=pl.CostEstimate(
            flops=2 * n**3, bytes_accessed=8 * 2**20, transcendentals=n
        ),
        name="latent_parts",
    )(*gram, *sketch, mix, before, activity)


def lag(block, carry):
    lane = lax.broadcasted_iota(jnp.int32, block.shape, 1)
    return jnp.where(lane == 0, carry, pltpu.roll(block, 1, 1))


def as_column(line):
    n = line.shape[1]
    square = (n, n)
    same = lax.broadcasted_iota(jnp.int32, square, 0) == lax.broadcasted_iota(jnp.int32, square, 1)
    return jnp.sum(jnp.where(same, line, 0.0), axis=1, keepdims=True)


def error_kernel(
    latents, signals, activity, maps, recurrent, bias,
    latents_out, frame_out, stats,
    last_latent, last_signal, cross, squares, hidden_squares,
):
    i = pl.program_id(0)
    rank = recurrent.shape[0]
    width = activity.shape[1]
    neurons = activity.shape[0]

    @pl.when(i == 0)
    def _():
        wide = last_latent.shape
        last_latent[...] = jnp.broadcast_to(as_column(latents[0, rank : rank + 1, :rank]), wide)
        last_signal[...] = jnp.broadcast_to(as_column(signals[0, rank : rank + 1, :rank]), wide)
        cross[...] = jnp.zeros_like(cross)
        squares[...] = jnp.zeros_like(squares)
        hidden_squares[...] = jnp.zeros_like(hidden_squares)

    latent = latents[0, :rank, :]
    signal = signals[0, :rank, :]
    latents_out[...] = latent
    lagged_latent = lag(latent, last_latent[:, :1])
    lagged_signal = lag(signal, last_signal[:, :1])
    last_latent[...] = jnp.broadcast_to(latent[:, width - 1 :], last_latent.shape)
    last_signal[...] = jnp.broadcast_to(signal[:, width - 1 :], last_signal.shape)
    hidden = jnp.tanh(product(recurrent[...], lagged_latent, 1, 0, precise) + bias[...])
    state = jnp.concatenate([hidden.astype(half), lagged_signal.astype(half)], axis=0)
    error = activity[...].astype(full) - product(maps[...], state, 1, 0)
    squared = error * error
    cross[...] += product(hidden, error, 1, 1, precise)
    frame_out[...] = jnp.sum(squared, axis=0, keepdims=True)
    total = squared[:, :BLOCK]
    hidden_square = hidden * hidden
    hidden_total = hidden_square[:, :BLOCK]
    for a in range(BLOCK, width, BLOCK):
        total = total + squared[:, a : a + BLOCK]
        hidden_total = hidden_total + hidden_square[:, a : a + BLOCK]
    squares[...] += total
    hidden_squares[...] += hidden_total

    @pl.when(i == pl.num_programs(0) - 1)
    def _():
        groups = neurons // BLOCK
        error_sq = product(jnp.ones((8, BLOCK), full), squares[...], 1, 1, precise)
        hidden_sq = jnp.sum(hidden_squares[...], axis=1, keepdims=True)
        stats[...] = jnp.zeros_like(stats)
        for g in range(groups):
            lanes = slice(g * BLOCK, (g + 1) * BLOCK)
            stats[:, g, :] = cross[:, lanes]
            stats[g, groups + 1 : groups + 2, :] = error_sq[:1, lanes]
        stats[:, groups, :] = jnp.broadcast_to(hidden_sq, (rank, BLOCK))


def error_stats(latents, signals, activity, maps, recurrent, bias):
    pieces, rows, width = latents.shape
    neurons, frames = activity.shape
    rank = recurrent.shape[0]
    whole = lambda i: (0, 0)
    return pl.pallas_call(
        error_kernel,
        grid=(pieces,),
        out_shape=(
            jax.ShapeDtypeStruct((rank, frames), full),
            jax.ShapeDtypeStruct((1, frames), full),
            jax.ShapeDtypeStruct((rank, neurons // BLOCK + 2, BLOCK), full),
        ),
        in_specs=[
            pl.BlockSpec((1, rows, width), lambda i: (i, 0, 0)),
            pl.BlockSpec((1, rows, width), lambda i: (i, 0, 0)),
            pl.BlockSpec((neurons, width), lambda i: (0, i)),
            pl.BlockSpec(maps.shape, whole),
            pl.BlockSpec(recurrent.shape, whole),
            pl.BlockSpec(bias.shape, whole),
        ],
        out_specs=(
            pl.BlockSpec((rank, width), lambda i: (0, i)),
            pl.BlockSpec((1, width), lambda i: (0, i)),
            pl.BlockSpec((rank, neurons // BLOCK + 2, BLOCK), lambda i: (0, 0, 0)),
        ),
        scratch_shapes=[
            pltpu.VMEM((rank, BLOCK), full),
            pltpu.VMEM((rank, BLOCK), full),
            pltpu.VMEM((rank, neurons), full),
            pltpu.VMEM((neurons, BLOCK), full),
            pltpu.VMEM((rank, BLOCK), full),
        ],
        compiler_params=pltpu.CompilerParams(vmem_limit_bytes=40 * 2**20),
        cost_estimate=pl.CostEstimate(
            flops=8 * neurons * frames * rank, bytes_accessed=8 * 2**20, transcendentals=rank * frames
        ),
        name="error_stats",
    )(latents, signals, activity, maps, recurrent, bias)


def score_kernel(frames_all, stats, out):
    groups = stats.shape[1] - 2
    hidden_sq = stats[:, groups, :]
    for g in range(groups):
        lanes = slice(g * BLOCK, (g + 1) * BLOCK)
        error_sq = stats[g, groups + 1 : groups + 2, :]
        out[:, lanes] = stats[:, g, :] / jnp.sqrt(
            frames_all * (error_sq / frames_all + epsilon) * (hidden_sq / frames_all + epsilon)
        )


def scores(stats, frames_all):
    rank, rows, _ = stats.shape
    return pl.pallas_call(
        functools.partial(score_kernel, float(frames_all)),
        out_shape=jax.ShapeDtypeStruct((rank, (rows - 2) * BLOCK), full),
        in_specs=in_vmem(1),
        out_specs=in_vmem(1)[0],
        name="scores",
    )(stats)


def region_tables(block_regions, region_mask, region_in, region_out):
    regions = region_mask.shape[0]
    signal_width = region_in.shape[1]
    block_total = block_regions.shape[0]
    block_rows = region_in.shape[0] // block_total
    onehot = (block_regions[:, None] == jnp.arange(regions, dtype=jnp.int32)[None, :]).astype(full)
    onehot = jnp.broadcast_to(onehot[:, None, :], (block_total, block_rows, regions)).reshape(
        block_total * block_rows, regions
    )
    allowed = jnp.dot(onehot, region_mask.astype(full), precision=precise)
    region_feed = (onehot[:, :, None] * region_in.astype(full)[:, None, :]).reshape(
        -1, regions * signal_width
    )
    spread = (allowed[:, :, None] * region_out.astype(full)[:, None, :]).reshape(
        -1, regions * signal_width
    )
    return (region_feed.astype(half), spread.astype(half))


def local(
    activity,
    test_matrix,
    basis_mix,
    recurrent,
    latent_bias,
    readout,
    region_in,
    region_out,
    region_of_block,
    region_mask,
):
    neurons_here, frames_here = activity.shape
    columns = test_matrix.shape[1] * lax.axis_size("region")
    chips = lax.axis_size("chip")
    slabs = chips * CORES
    regions = lax.axis_size("region")
    core = lax.axis_index("core")

    test_full = lax.all_gather(test_matrix.T, "region", axis=0, tiled=True)
    before = lax.ppermute(activity[:, -1], SLAB, [(i, i + 1) for i in range(slabs - 1)])
    before = jnp.broadcast_to(before[None, :], (16, neurons_here))

    block_count = neurons_here // BLOCK
    my_blocks = lax.dynamic_slice_in_dim(
        region_of_block, lax.axis_index("region") * block_count, block_count
    )
    region_feed, spread = region_tables(my_blocks, region_mask, region_in, region_out)
    maps = jnp.concatenate([readout, spread], axis=1)
    rank = region_feed.shape[1]
    signal = product(region_feed, activity, 0, 0)
    signal = signal.reshape(rank, regions, -1).transpose(1, 0, 2)
    prior = jnp.pad(product(before[:8], region_feed, 1, 0), ((0, 0), (0, signal.shape[2] - rank)))
    prior = jnp.broadcast_to(prior[None], (regions,) + prior.shape)
    signal = jnp.concatenate([signal, prior], axis=1)
    signal, test_full = lax.optimization_barrier((signal, test_full))
    signals = lax.psum(signal, "region")

    mid = columns // CORES
    theirs = product(lax.dynamic_slice_in_dim(test_full, (1 - core) * mid, mid), activity, 1, 1)
    mine = product(lax.dynamic_slice_in_dim(test_full, core * mid, mid), activity, 1, 1)
    mine = mine + other_core(theirs)
    own = scatter_sum(mine.reshape(chips, mid // chips, neurons_here), "chip")
    mine = share(own, "chip").reshape(mid, neurons_here)
    sketch = in_core_order(mine, other_core(mine))

    rows = jnp.concatenate([product(own, part, 1, 1, precise) for part in sketch], axis=1)
    rows = jnp.sum(share(rows, "region"), axis=0)
    mine = share(rows, "chip").reshape(mid, columns)
    gram = in_core_order(mine, other_core(mine))

    parts = latent_parts(gram, sketch, basis_mix.T, before, activity, regions)
    latents = share(scatter_sum(parts, "region"), "region")
    latents_out, frame_sq, stats = error_stats(
        latents, signals, activity, maps, recurrent, latent_bias[:, None]
    )
    frame_sq = lax.psum(frame_sq.reshape(frames_here), "region")
    stats = stats.reshape((slabs, rank // slabs) + stats.shape[1:])
    stats = share(scatter_sum(stats, SLAB), SLAB)
    stats = stats.reshape((rank,) + stats.shape[2:])
    score = scores(stats, frames_here * slabs)
    return (latents_out, frame_sq / (neurons_here * regions), score.T)


def solution(mesh):
    slabs, regions = mesh.devices.shape
    devices = mesh.devices.reshape(slabs // CORES, CORES, regions)
    mesh = Mesh(devices, ("chip", "core", "region"))
    in_specs = (
        P("region", SLAB),
        P(SLAB, "region"),
        P(),
        P(),
        P(),
        P("region", None),
        P("region", None),
        P("region", None),
        P(),
        P(),
    )
    out_specs = (P(None, SLAB), P(SLAB), P("region", None))
    return jax.shard_map(local, mesh=mesh, in_specs=in_specs, out_specs=out_specs, check_vma=False)
```

time: 1060 us -> 379 us (0.36); the launches traced: 1050 us -> 378 us
  waiting for transfers between devices: 428 us -> 121 us
  blocking collectives: 326 us -> 156 us
  other arithmetic: 130 us -> 8.45 us
  local copies, waits for them, and re-layouts: 52.3 us -> 12.2 us
  Pallas kernels: 0 us -> 36.8 us
  starting transfers between devices: 55 us -> 18.6 us
  matrix products: 39.4 us -> 11.3 us
    psum x3 -> x1, waiting for transfers between devices: 372 us -> 76.8 us  [local(): signals = lax.psum(signal, 'region')]
    psum x3 -> x1, blocking collectives: 163 us -> 16.7 us  [local(): frame_sq = lax.psum(frame_sq.reshape(frames_here), 'region')]
    all_to_all x0 -> x6, blocking collectives: none -> 139 us  [the longest x3 76.2 us: scatter_sum(): return jnp.sum(lax.all_to_all(pieces, axis, 0, 0), axis=0)]
    another operation x17 -> x0, other arithmetic: 125 us -> none  [the longest x14 82.5 us: orthonormal(): lower = jnp.linalg.cholesky(gram)]
    unnamed x1 -> x0, blocking collectives: 120 us -> none
    unnamed x16 -> x0, starting transfers between devices: 50.7 us -> none
    all_gather x1 -> x0, blocking collectives: 43.4 us -> none  [local(): lax.all_gather(loading_rows, 'tm', axis=0, tiled=True)]
    pallas_call x0 -> x3, Pallas kernels: none -> 36.8 us  [the longest x1 22 us: latent_parts(): pl.pallas_call(latents_kernel, out_shape=jax.ShapeDtypeStruct((pieces, ra...]
  transfers between devices with their start and end apart: 22 -> 8, of which waited for: 8 -> 6; matrix products, arithmetic and copies ran while one was open for 1% -> 4% of each run, Pallas kernels for 0% -> 0%
where the time goes in v1:
time: 379 us; the launch traced here: 378 us
  blocking collectives  156 us (41%)
  waiting for transfers between devices  121 us (32%)
  Pallas kernels  36.8 us (10%)
  starting transfers between devices  18.6 us (5%)
  between operations  14.3 us (4%)
  local copies, waits for them, and re-layouts  12.2 us (3%)
  matrix products  11.3 us (3%)
  other arithmetic  8.45 us (2%)
    psum x1, waiting for transfers between devices, local(): signals = lax.psum(signal, 'region')  76.8 us
    all_to_all x3, blocking collectives, scatter_sum(): return jnp.sum(lax.all_to_all(pieces, axis, 0, 0), axis=0)  76.2 us
    all_to_all x3, blocking collectives, share(): return lax.all_to_all(lax.optimization_barrier(copies), axis, 0, 0)  62.8 us
    all_gather x1, waiting for transfers between devices, local(): test_full = lax.all_gather(test_matrix.T, 'region', axis=0, tiled=True)  35.2 us
    pallas_call x1, Pallas kernels, latent_parts(): pl.pallas_call(latents_kernel, out_shape=jax.ShapeDtypeStruct((pieces, ra...  22 us
    psum x1, blocking collectives, local(): frame_sq = lax.psum(frame_sq.reshape(frames_here), 'region')  16.7 us
    pallas_call x1, Pallas kernels, error_stats(): pl.pallas_call(error_kernel, grid=(pieces,), out_shape=(jax.ShapeDtypeStr...  12.9 us
    dot_general x6, matrix products, product(): lax.dot_general(a, b, (((ca,), (cb,)), ((), ())), precision=precision, pr...  11.1 us
  transfers between devices with their start and end apart: 8, of which 6 were waited for; matrix products, arithmetic and copies ran while one was open for 4% of the time, Pallas kernels for 0%

profile of v1, /device:TPU:6, one launch (start us, length us, event | category | flops | bytes accessed | tf_op | source)
XLA Modules:
  0.0 378.1 jit_solution(16469830444665106391)
XLA Ops:
  9.1 1.9 collective-permute-start
  11.7 4.7 %copy.32 = bf16[2048,768]{1,0:T(8,128)(2,1)} copy(bf16[2048,768]{0,1:T(8,128)(2,1)} %bitcast.43) | data formatting | bytes 6291456 | tf_op jit(solution)/shard_map/dot_general | solution.py:22
  16.6 3.9 %convolution_bitcast_fusion = f32[8,64,256]{2,1,0:T(8,128)} fusion(bf16[8,256,768]{2,1,0:T(8,128)(2,1)} %bitcast.47, f32[768,8]{0,1:T(8,128)S(1)} %convert_element_type.38, f32[768,8]{0,1:T(8,128)S(1)} %broadcast_bitcast_fusion), kind=kOutput, calls=%fused_computation.2 | convolution fusion | flops 201424896 | bytes 3719168 | tf_op jit(solution)/shard_map/dot_general | solution.py:22
  21.1 1.9 pad_maximum_fusion
  23.0 35.2 %all-gather.2.cloned.1.call-done = bf16[512,2048]{1,0:T(8,128)(2,1)} async-done(((bf16[64,2048]{1,0:T(8,128)(2,1)}), bf16[512,2048]{1,0:T(8,128)(2,1)}) %all-gather.2.cloned.1.call-update) | async-done | bytes 2097168 | tf_op jit(solution)/shard_map/all_gather | solution.py:319
  58.2 3.2 fusion.1
  61.4 1.9 collective-permute-start.1
  63.3 2.6 collective-permute-done.1
  65.9 2.5 fusion
  68.4 31.1 %all_to_all.40 = f32[32,8,768]{2,1,0:T(8,128)} all-to-all(f32[32,8,768]{2,1,0:T(8,128)S(1)} %fusion), channel_id=1, replica_groups=mesh['chip'=32,'core'=2,'region'=8] {'chip'}, dimensions={0} | all-to-all | bytes 1572864 | tf_op jit(solution)/shard_map/all_to_all | solution.py:32
  100.7 28.4 %all_to_all.41 = f32[32,8,768]{2,1,0:T(8,128)} all-to-all(f32[32,8,768]{2,1,0:T(8,128)S(1)} %broadcast_in_dim.20), channel_id=1, replica_groups=mesh['chip'=32,'core'=2,'region'=8] {'chip'}, dimensions={0} | all-to-all | bytes 1572864 | tf_op jit(solution)/shard_map/all_to_all | solution.py:37
  129.1 1.9 collective-permute-start.2
  131.0 2.6 collective-permute-done.2
  137.5 13.8 %all_to_all.42 = f32[8,8,512]{2,1,0:T(8,128)S(1)} all-to-all(f32[8,8,512]{2,1,0:T(8,128)S(1)} %broadcast_in_dim.21), channel_id=1, replica_groups=mesh['chip'=32,'core'=2,'region'=8] {'region'}, dimensions={0} | all-to-all | bytes 262144 | tf_op jit(solution)/shard_map/all_to_all | solution.py:37
  151.4 20.6 %all_to_all.43 = f32[32,8,512]{2,1,0:T(8,128)S(1)} all-to-all(f32[32,8,512]{2,1,0:T(8,128)S(1)} %broadcast_in_dim.22), channel_id=1, replica_groups=mesh['chip'=32,'core'=2,'region'=8] {'chip'}, dimensions={0} | all-to-all | bytes 1048576 | tf_op jit(solution)/shard_map/all_to_all | solution.py:37
  172.0 2.1 collective-permute-start.3
  176.0 22.0 %latent_parts.1 = f32[8,72,256]{2,1,0:T(8,128)S(1)} custom-call(f32[256,512]{1,0:T(8,128)S(1)} %get-tuple-element.16.gram_low, f32[256,512]{1,0:T(8,128)S(1)} %get-tuple-element.15.gram_high, f32[256,768]{1,0:T(8,128)S(1)} %copy-done.2, f32[256,768]{1,0:T(8,128)S(1)} %copy-done.4, f32[64,512]{1,0:T(8,128)S(1)} %bitcast.45, ...), custom_call_target="tpu_custom_call" | custom-call | flops 268435456 | bytes 8388608 | tf_op jit(solution)/shard_map/latent_parts/pallas_call | solution.py:134
  198.1 22.7 %all_to_all.44 = f32[8,72,256]{2,1,0:T(8,128)} all-to-all(f32[8,72,256]{2,1,0:T(8,128)S(1)} %latent_parts.1), channel_id=1, replica_groups=mesh['chip'=32,'core'=2,'region'=8] {'region'}, dimensions={0} | all-to-all | bytes 1179648 | tf_op jit(solution)/shard_map/all_to_all | solution.py:32
  222.7 4.2 %all-to-all-start.5 = ((f32[8,72,256]{2,1,0:T(8,128)}), f32[8,72,256]{2,1,0:T(8,128)}, u32[]{:S(2)}, u32[]{:S(2)}) async-start(f32[8,72,256]{2,1,0:T(8,128)} %broadcast_in_dim.24), calls=%async_computation.5 | async-start | bytes 1179648 | tf_op jit(solution)/shard_map/all_to_all | solution.py:37
  230.9 76.8 %all-reduce.3.cloned.1.call-done.signals = f32[8,72,256]{2,1,0:T(8,128)} async-done(((f32[8,72,256]{2,1,0:T(8,128)}), f32[8,72,256]{2,1,0:T(8,128)}) %all-reduce.3.cloned.1.call-update) | async-done | bytes 589840 | tf_op jit(solution)/shard_map/psum | solution.py:336
  308.8 12.9 %error_stats.1 = (f32[64,2048]{1,0:T(8,128)}, f32[1,2048]{1,0:T(1,128)S(1)}, f32[64,8,128]{2,1,0:T(8,128)S(1)}) custom-call(f32[8,72,256]{2,1,0:T(8,128)} %all-to-all-done.5.latents, f32[8,72,256]{2,1,0:T(8,128)S(1)} %copy-done.5, bf16[768,2048]{1,0:T(8,128)(2,1)S(1)} %copy-done, bf16[768,128]{1,0:T(8,128)(2,1)S(1)} %pad_maximum_fusion.1.maps, ...), custom_call_target="tpu_custom_call" | custom-call | flops 805306368 | bytes 8388608 | tf_op jit(solution)/shard_map/error_stats/pallas_call | solution.py:223
  321.7 22.4 %all_to_all.45 = f32[64,1,8,128]{3,2,1,0:T(8,128)S(1)} all-to-all(f32[64,1,8,128]{3,2,1,0:T(8,128)S(1)} %bitcast.44), channel_id=1, replica_groups=mesh['chip'=32,'core'=2,'region'=8] {'chip','core'}, dimensions={0} | all-to-all | bytes 524288 | tf_op jit(solution)/shard_map/all_to_all | solution.py:32
  345.0 6.5 %all-to-all-start.7 = ((f32[64,1,8,128]{3,2,1,0:T(8,128)}), f32[64,1,8,128]{3,2,1,0:T(8,128)S(1)}, u32[]{:S(2)}, u32[]{:S(2)}) async-start(f32[64,1,8,128]{3,2,1,0:T(8,128)} %broadcast_in_dim.26), calls=%async_computation.7 | async-start | bytes 524288 | tf_op jit(solution)/shard_map/all_to_all | solution.py:37
  351.4 16.7 %psum.15 = f32[2048]{0:T(1024)S(1)} all-reduce(f32[2048]{0:T(1024)S(1)} %bitcast.46), channel_id=1, replica_groups=mesh['chip'=32,'core'=2,'region'=8] {'region'}, use_global_device_ids=true, to_apply=%region_4.5 | all-reduce | flops 2048 | bytes 16384 | tf_op jit(solution)/shard_map/psum | solution.py:356
  (68 shorter events, 21.3 us)
Async XLA Ops:
  7.2 51.1 %all-gather.2.cloned.1.call-start = ((), (), s32[]{:S(2)}) async-start(), calls=%async_computation.8 | async-start | bytes 2359296 | tf_op jit(solution)/shard_map/all_gather | solution.py:319
  9.1 11.9 %collective-permute-start = (bf16[768]{0:T(1024)(128)(2,1)S(1)}, bf16[768]{0:T(1024)(128)(2,1)S(1)}, u32[]{:S(2)}, u32[]{:S(2)}) collective-permute-start(bf16[768]{0:T(1024)(128)(2,1)S(1)} %slice_reduce_fusion), channel_id=1, source_target_pairs={{0,8},{8,16},{16,24},{24,32},{32,40},{40,48},{48,56},{56,64},{64,7... | collective-permute-start | bytes 4616 | tf_op jit(solution)/shard_map/ppermute | solution.py:320
  11.7 4.7 %copy-start.13 = (s32[48]{0:T(128)S(1)}, s32[48]{0:T(128)}, u32[]{:S(2)}) copy-start(s32[48]{0:T(128)} %param.18) | copy-start | bytes 580
  16.4 41.9 %copy-start = (bf16[768,2048]{1,0:T(8,128)(2,1)S(1)}, bf16[768,2048]{1,0:T(8,128)(2,1)}, u32[]{:S(2)}) copy-start(bf16[768,2048]{1,0:T(8,128)(2,1)} %activity.3) | copy-start | bytes 9437188
  61.4 4.5 %collective-permute-start.1 = (f32[256,768]{1,0:T(8,128)}, f32[256,768]{1,0:T(8,128)}, u32[]{:S(2)}, u32[]{:S(2)}) collective-permute-start(f32[256,768]{1,0:T(8,128)} %fusion.1), channel_id=1, source_target_pairs={{0,8},{8,0},{1,9},{9,1},{2,10},{10,2},{3,11},{11,3},{4,12},{12,4},... | collective-permute-start | bytes 2359304 | tf_op jit(solution)/shard_map/ppermute | solution.py:28
  129.1 4.5 %collective-permute-start.2 = (f32[256,768]{1,0:T(8,128)}, f32[256,768]{1,0:T(8,128)}, u32[]{:S(2)}, u32[]{:S(2)}) collective-permute-start(f32[256,768]{1,0:T(8,128)} %bitcast.9), channel_id=1, source_target_pairs={{0,8},{8,0},{1,9},{9,1},{2,10},{10,2},{3,11},{11,3},{4,12},{12,4},... | collective-permute-start | bytes 2359304 | tf_op jit(solution)/shard_map/ppermute | solution.py:28
  135.1 1.7 copy-start.3
  135.1 40.9 %copy-start.6 = (f32[512,64]{0,1:T(8,128)S(1)}, f32[512,64]{0,1:T(8,128)}, u32[]{:S(2)}) copy-start(f32[512,64]{0,1:T(8,128)} %param.12) | copy-start | bytes 393220
  135.8 0.9 copy-start.1
  151.3 24.7 %copy-start.2 = (f32[256,768]{1,0:T(8,128)S(1)}, f32[256,768]{1,0:T(8,128)}, u32[]{:S(2)}) copy-start(f32[256,768]{1,0:T(8,128)} %copy-done.1) | copy-start | bytes 2359300
  151.3 24.7 %copy-start.4 = (f32[256,768]{1,0:T(8,128)S(1)}, f32[256,768]{1,0:T(8,128)}, u32[]{:S(2)}) copy-start(f32[256,768]{1,0:T(8,128)} %copy-done.3) | copy-start | bytes 2359300
  172.0 3.8 %collective-permute-start.3 = (f32[256,512]{1,0:T(8,128)S(1)}, f32[256,512]{1,0:T(8,128)S(1)}, u32[]{:S(2)}, u32[]{:S(2)}) collective-permute-start(f32[256,512]{1,0:T(8,128)S(1)} %bitcast.48), channel_id=1, source_target_pairs={{0,8},{8,0},{1,9},{9,1},{2,10},{10,2},{3,11},{11,3},{4,12},{12,4},... | collective-permute-start | bytes 1572872 | tf_op jit(solution)/shard_map/ppermute | solution.py:28
  198.0 29.7 %copy-start.10 = (bf16[768,8]{0,1:T(8,128)(2,1)S(1)}, bf16[768,8]{0,1:T(8,128)(2,1)}, u32[]{:S(2)}) copy-start(bf16[768,8]{0,1:T(8,128)(2,1)} %param.17) | copy-start | bytes 36868
  198.0 29.7 %copy-start.12 = (s32[8,8]{1,0:T(8,128)S(1)}, s32[8,8]{1,0:T(8,128)}, u32[]{:S(2)}) copy-start(s32[8,8]{1,0:T(8,128)} %param.19) | copy-start | bytes 772
  198.0 30.8 %copy-start.9 = (bf16[768,64]{0,1:T(8,128)(2,1)S(1)}, bf16[768,64]{0,1:T(8,128)(2,1)}, u32[]{:S(2)}) copy-start(bf16[768,64]{0,1:T(8,128)(2,1)} %param.15) | copy-start | bytes 294916
  198.1 31.6 %copy-start.11 = (f32[64]{0:T(128)S(1)}, f32[64]{0:T(128)}, u32[]{:S(2)}) copy-start(f32[64]{0:T(128)} %param.14) | copy-start | bytes 772
  198.1 109.6 %copy-start.7 = (f32[64,64]{1,0:T(8,128)S(1)}, f32[64,64]{1,0:T(8,128)}, u32[]{:S(2)}) copy-start(f32[64,64]{1,0:T(8,128)} %recurrent.1) | copy-start | bytes 49156
  222.7 85.0 %all-to-all-start.5 = ((f32[8,72,256]{2,1,0:T(8,128)}), f32[8,72,256]{2,1,0:T(8,128)}, u32[]{:S(2)}, u32[]{:S(2)}) async-start(f32[8,72,256]{2,1,0:T(8,128)} %broadcast_in_dim.24), calls=%async_computation.5 | async-start | bytes 1179648 | tf_op jit(solution)/shard_map/all_to_all | solution.py:37
  226.9 80.8 %all-reduce.3.cloned.1.call-start = ((), (), s32[]{:S(2)}) async-start(), calls=%async_computation.9 | async-start | bytes 1179648 | tf_op jit(solution)/shard_map/psum | solution.py:336
  307.7 1.1 copy-start.5
  345.0 23.8 %all-to-all-start.7 = ((f32[64,1,8,128]{3,2,1,0:T(8,128)}), f32[64,1,8,128]{3,2,1,0:T(8,128)S(1)}, u32[]{:S(2)}, u32[]{:S(2)}) async-start(f32[64,1,8,128]{3,2,1,0:T(8,128)} %broadcast_in_dim.26), calls=%async_computation.7 | async-start | bytes 524288 | tf_op jit(solution)/shard_map/all_to_all | solution.py:37
  368.7 0.7 copy-start.8
Sparse Core Ops, SparseCore 0:
  10.1 48.1 all-gather.1
  230.1 77.5 all-reduce.2

commit v2 on v1

--- a/solution.py
+++ b/solution.py
@@ -161,92 +161,83 @@
     return jnp.sum(jnp.where(same, line, 0.0), axis=1, keepdims=True)
 
 
+def split(x):
+    high = x.astype(half)
+    return high, (x - high.astype(full)).astype(half)
+
+
 def error_kernel(
     latents, signals, activity, maps, recurrent, bias,
-    latents_out, frame_out, stats,
-    last_latent, last_signal, cross, squares, hidden_squares,
+    latents_out, frame_out, stats, cross, cross_low, squares,
 ):
-    i = pl.program_id(0)
+    pieces, _, width = latents.shape
     rank = recurrent.shape[0]
-    width = activity.shape[1]
     neurons = activity.shape[0]
-
-    @pl.when(i == 0)
-    def _():
-        wide = last_latent.shape
-        last_latent[...] = jnp.broadcast_to(as_column(latents[0, rank : rank + 1, :rank]), wide)
-        last_signal[...] = jnp.broadcast_to(as_column(signals[0, rank : rank + 1, :rank]), wide)
-        cross[...] = jnp.zeros_like(cross)
-        squares[...] = jnp.zeros_like(squares)
-        hidden_squares[...] = jnp.zeros_like(hidden_squares)
-
-    latent = latents[0, :rank, :]
-    signal = signals[0, :rank, :]
-    latents_out[...] = latent
-    lagged_latent = lag(latent, last_latent[:, :1])
-    lagged_signal = lag(signal, last_signal[:, :1])
-    last_latent[...] = jnp.broadcast_to(latent[:, width - 1 :], last_latent.shape)
-    last_signal[...] = jnp.broadcast_to(signal[:, width - 1 :], last_signal.shape)
-    hidden = jnp.tanh(product(recurrent[...], lagged_latent, 1, 0, precise) + bias[...])
-    state = jnp.concatenate([hidden.astype(half), lagged_signal.astype(half)], axis=0)
-    error = activity[...].astype(full) - product(maps[...], state, 1, 0)
-    squared = error * error
-    cross[...] += product(hidden, error, 1, 1, precise)
-    frame_out[...] = jnp.sum(squared, axis=0, keepdims=True)
-    total = squared[:, :BLOCK]
-    hidden_square = hidden * hidden
-    hidden_total = hidden_square[:, :BLOCK]
-    for a in range(BLOCK, width, BLOCK):
-        total = total + squared[:, a : a + BLOCK]
-        hidden_total = hidden_total + hidden_square[:, a : a + BLOCK]
-    squares[...] += total
-    hidden_squares[...] += hidden_total
-
-    @pl.when(i == pl.num_programs(0) - 1)
-    def _():
-        groups = neurons // BLOCK
-        error_sq = product(jnp.ones((8, BLOCK), full), squares[...], 1, 1, precise)
-        hidden_sq = jnp.sum(hidden_squares[...], axis=1, keepdims=True)
-        stats[...] = jnp.zeros_like(stats)
-        for g in range(groups):
-            lanes = slice(g * BLOCK, (g + 1) * BLOCK)
-            stats[:, g, :] = cross[:, lanes]
-            stats[g, groups + 1 : groups + 2, :] = error_sq[:1, lanes]
-        stats[:, groups, :] = jnp.broadcast_to(hidden_sq, (rank, BLOCK))
+    groups = neurons // BLOCK
+    last_latent = as_column(latents[0, rank : rank + 1, :rank])
+    last_signal = as_column(signals[0, rank : rank + 16, :].astype(full)[:1, :rank])
+    hidden_total = jnp.zeros((rank, BLOCK), full)
+    for i in range(pieces):
+        frames = slice(i * width, (i + 1) * width)
+        latent = latents[i, :rank, :]
+        signal = signals[i, :rank, :].astype(full)
+        latents_out[:, frames] = latent
+        lagged_latent = lag(latent, last_latent)
+        lagged_signal = lag(signal, last_signal)
+        last_latent = latent[:, width - 1 :]
+        last_signal = signal[:, width - 1 :]
+        hidden = jnp.tanh(product(recurrent[...], lagged_latent, 1, 0, precise) + bias[...])
+        high, low = split(hidden)
+        state = jnp.concatenate([high, lagged_signal.astype(half)], axis=0)
+        both = jnp.concatenate([high, low], axis=0)
+        error = activity[:, frames].astype(full) - product(maps[...], state, 1, 0)
+        error_high, error_low = split(error)
+        by_both = product(error_high, both, 1, 1)
+        by_high = product(error_low, high, 1, 1)
+        squared = error * error
+        frame_out[:, frames] = jnp.sum(squared, axis=0, keepdims=True)
+        total = squared[:, :BLOCK]
+        hidden_square = hidden * hidden
+        for a in range(0, width, BLOCK):
+            if a:
+                total = total + squared[:, a : a + BLOCK]
+            hidden_total = hidden_total + hidden_square[:, a : a + BLOCK]
+        if i:
+            cross[...] += by_both
+            cross_low[...] += by_high
+            squares[...] += total
+        else:
+            cross[...] = by_both
+            cross_low[...] = by_high
+            squares[...] = total
+    error_sq = product(jnp.ones((8, BLOCK), full), squares[...], 1, 1, precise)
+    hidden_sq = jnp.sum(hidden_total, axis=1, keepdims=True)
+    stats[:, groups:, :] = jnp.zeros((rank, 2, BLOCK), full)
+    for g in range(groups):
+        lanes = slice(g * BLOCK, (g + 1) * BLOCK)
+        by_both = cross[lanes, :].T
+        by_high = cross_low[lanes, :].T
+        stats[:, g, :] = by_both[:rank, :] + by_both[rank:, :] + by_high
+        stats[g, groups + 1 : groups + 2, :] = error_sq[:1, lanes]
+    stats[:, groups, :] = jnp.broadcast_to(hidden_sq, (rank, BLOCK))
 
 
 def error_stats(latents, signals, activity, maps, recurrent, bias):
-    pieces, rows, width = latents.shape
     neurons, frames = activity.shape
     rank = recurrent.shape[0]
-    whole = lambda i: (0, 0)
     return pl.pallas_call(
         error_kernel,
-        grid=(pieces,),
         out_shape=(
             jax.ShapeDtypeStruct((rank, frames), full),
             jax.ShapeDtypeStruct((1, frames), full),
             jax.ShapeDtypeStruct((rank, neurons // BLOCK + 2, BLOCK), full),
         ),
-        in_specs=[
-            pl.BlockSpec((1, rows, width), lambda i: (i, 0, 0)),
-            pl.BlockSpec((1, rows, width), lambda i: (i, 0, 0)),
-            pl.BlockSpec((neurons, width), lambda i: (0, i)),
-            pl.BlockSpec(maps.shape, whole),
-            pl.BlockSpec(recurrent.shape, whole),
-            pl.BlockSpec(bias.shape, whole),
-        ],
-        out_specs=(
-            pl.BlockSpec((rank, width), lambda i: (0, i)),
-            pl.BlockSpec((1, width), lambda i: (0, i)),
-            pl.BlockSpec((rank, neurons // BLOCK + 2, BLOCK), lambda i: (0, 0, 0)),
-        ),
+        in_specs=in_vmem(6),
+        out_specs=tuple(in_vmem(3)),
         scratch_shapes=[
-            pltpu.VMEM((rank, BLOCK), full),
-            pltpu.VMEM((rank, BLOCK), full),
-            pltpu.VMEM((rank, neurons), full),
+            pltpu.VMEM((neurons, 2 * rank), full),
+            pltpu.VMEM((neurons, rank), full),
             pltpu.VMEM((neurons, BLOCK), full),
-            pltpu.VMEM((rank, BLOCK), full),
         ],
         compiler_params=pltpu.CompilerParams(vmem_limit_bytes=40 * 2**20),
         cost_estimate=pl.CostEstimate(
@@ -329,11 +320,15 @@
     rank = region_feed.shape[1]
     signal = product(region_feed, activity, 0, 0)
     signal = signal.reshape(rank, regions, -1).transpose(1, 0, 2)
-    prior = jnp.pad(product(before[:8], region_feed, 1, 0), ((0, 0), (0, signal.shape[2] - rank)))
+    prior = product(before, region_feed, 1, 0)
+    prior = jnp.pad(prior, ((0, 0), (0, signal.shape[2] - rank)))
     prior = jnp.broadcast_to(prior[None], (regions,) + prior.shape)
-    signal = jnp.concatenate([signal, prior], axis=1)
-    signal, test_full = lax.optimization_barrier((signal, test_full))
-    signals = lax.psum(signal, "region")
+    signal = scatter_sum(jnp.concatenate([signal, prior], axis=1), "region")
+    signals = share(signal.astype(half), "region")
+    bias = latent_bias[:, None]
+    test_full, signals, maps, before, bias = lax.optimization_barrier(
+        (test_full, signals, maps, before, bias)
+    )
 
     mid = columns // CORES
     theirs = product(lax.dynamic_slice_in_dim(test_full, (1 - core) * mid, mid), activity, 1, 1)
@@ -351,7 +346,7 @@
     parts = latent_parts(gram, sketch, basis_mix.T, before, activity, regions)
     latents = share(scatter_sum(parts, "region"), "region")
     latents_out, frame_sq, stats = error_stats(
-        latents, signals, activity, maps, recurrent, latent_bias[:, None]
+        latents, signals, activity, maps, recurrent, bias
     )
     frame_sq = lax.psum(frame_sq.reshape(frames_here), "region")
     stats = stats.reshape((slabs, rank // slabs) + stats.shape[1:])

time: 379 us -> 326 us (0.86)
  waiting for transfers between devices: 121 us -> 40 us
  blocking collectives: 156 us -> 185 us
  Pallas kernels: 36.8 us -> 30.3 us
    psum x1 -> x0, waiting for transfers between devices: 76.8 us -> none  [local(): signals = lax.psum(signal, 'region')]
    all_gather x1, waiting for transfers between devices: 35.2 us -> 0.01 us  [local(): test_full = lax.all_gather(test_matrix.T, 'region', axis=0, tiled=True)]
    all_to_all x3 -> x4, blocking collectives: 76.2 us -> 108 us  [scatter_sum(): return jnp.sum(lax.all_to_all(pieces, axis, 0, 0), axis=0)]
    all_to_all x2 -> x3, waiting for transfers between devices: 0.01 us -> 27.7 us  [share(): return lax.all_to_all(lax.optimization_barrier(copies), axis, 0, 0)]
    pallas_call x1, Pallas kernels: 12.9 us -> 6.47 us  [error_stats(): pl.pallas_call(error_kernel, out_shape=(jax.ShapeDtypeStruct((rank, frame...]
    ppermute x1, waiting for transfers between devices: 0.49 us -> 4.73 us  [local(): lax.ppermute(activity[:, -1], SLAB, [(i, i + 1) for i in range(slabs - 1)])]
    all_to_all x2 -> x3, starting transfers between devices: 10.7 us -> 14.1 us  [share(): return lax.all_to_all(lax.optimization_barrier(copies), axis, 0, 0)]
  transfers between devices with their start and end apart: 8 -> 8, of which waited for: 6 -> 6; matrix products, arithmetic and copies ran while one was open for 4% -> 5% of each run, Pallas kernels for 0% -> 0%
where the time goes in v2:
time: 326 us; the launch traced here: 324 us
  blocking collectives  185 us (57%)
  waiting for transfers between devices  40 us (12%)
  Pallas kernels  30.3 us (9%)
  starting transfers between devices  22 us (7%)
  between operations  14.4 us (4%)
  local copies, waits for them, and re-layouts  14 us (4%)
  other arithmetic  10.6 us (3%)
  matrix products  8.45 us (3%)
    all_to_all x4, blocking collectives, scatter_sum(): return jnp.sum(lax.all_to_all(pieces, axis, 0, 0), axis=0)  108 us
    all_to_all x3, blocking collectives, share(): return lax.all_to_all(lax.optimization_barrier(copies), axis, 0, 0)  62.1 us
    all_to_all x3, waiting for transfers between devices, share(): return lax.all_to_all(lax.optimization_barrier(copies), axis, 0, 0)  27.7 us
    pallas_call x1, Pallas kernels, latent_parts(): pl.pallas_call(latents_kernel, out_shape=jax.ShapeDtypeStruct((pieces, ra...  22 us
    psum x1, blocking collectives, local(): frame_sq = lax.psum(frame_sq.reshape(frames_here), 'region')  15 us
    all_to_all x3, starting transfers between devices, share(): return lax.all_to_all(lax.optimization_barrier(copies), axis, 0, 0)  14.1 us
    dot_general x6, matrix products, product(): lax.dot_general(a, b, (((ca,), (cb,)), ((), ())), precision=precision, pr...  8.21 us
    ppermute x3, waiting for transfers between devices, other_core(): return lax.ppermute(x, 'core', [(0, 1), (1, 0)])  6.87 us
  transfers between devices with their start and end apart: 8, of which 6 were waited for; matrix products, arithmetic and copies ran while one was open for 5% of the time, Pallas kernels for 0%

profile of v2, /device:TPU:6, one launch (start us, length us, event | category | flops | bytes accessed | tf_op | source)
XLA Modules:
  0.0 324.2 jit_solution(8518951665503412281)
XLA Ops:
  9.1 1.9 collective-permute-start
  11.7 3.2 copy.32
  16.2 4.7 %collective-permute-done = bf16[768]{0:T(1024)(128)(2,1)S(1)} collective-permute-done((bf16[768]{0:T(1024)(128)(2,1)S(1)}, bf16[768]{0:T(1024)(128)(2,1)S(1)}, u32[]{:S(2)}, u32[]{:S(2)}) %collective-permute-start) | collective-permute-done | bytes 1568 | tf_op jit(solution)/shard_map/ppermute | solution.py:311
  21.2 32.9 %all_to_all.50 = f32[8,80,256]{2,1,0:T(8,128)} all-to-all(f32[8,80,256]{2,1,0:T(8,128)S(1)} %pad_maximum_fusion), channel_id=1, replica_groups=mesh['chip'=32,'core'=2,'region'=8] {'region'}, dimensions={0} | all-to-all | bytes 1310720 | tf_op jit(solution)/shard_map/all_to_all | solution.py:32
  56.0 3.4 %all-to-all-start.1 = ((bf16[8,80,256]{2,1,0:T(8,128)(2,1)}), bf16[8,80,256]{2,1,0:T(8,128)(2,1)S(1)}, u32[]{:S(2)}, u32[]{:S(2)}) async-start(bf16[8,80,256]{2,1,0:T(8,128)(2,1)} %broadcast_in_dim.23), calls=%async_computation.1 | async-start | bytes 655360 | tf_op jit(solution)/shard_map/all_to_all | solution.py:37
  65.6 8.4 %all-to-all-done.1.signals = bf16[8,80,256]{2,1,0:T(8,128)(2,1)S(1)} async-done(((bf16[8,80,256]{2,1,0:T(8,128)(2,1)}), bf16[8,80,256]{2,1,0:T(8,128)(2,1)S(1)}, u32[]{:S(2)}, u32[]{:S(2)}) %all-to-all-start.1) | async-done | bytes 327712 | tf_op jit(solution)/shard_map/all_to_all | solution.py:37
  74.0 3.1 fusion.1
  79.1 2.6 collective-permute-done.1
  81.7 2.5 fusion
  84.1 32.9 %all_to_all.51 = f32[32,8,768]{2,1,0:T(8,128)} all-to-all(f32[32,8,768]{2,1,0:T(8,128)S(1)} %fusion), channel_id=1, replica_groups=mesh['chip'=32,'core'=2,'region'=8] {'chip'}, dimensions={0} | all-to-all | bytes 1572864 | tf_op jit(solution)/shard_map/all_to_all | solution.py:32
  118.2 28.4 %all_to_all.52 = f32[32,8,768]{2,1,0:T(8,128)} all-to-all(f32[32,8,768]{2,1,0:T(8,128)S(1)} %broadcast_in_dim.25), channel_id=1, replica_groups=mesh['chip'=32,'core'=2,'region'=8] {'chip'}, dimensions={0} | all-to-all | bytes 1572864 | tf_op jit(solution)/shard_map/all_to_all | solution.py:37
  146.7 1.9 collective-permute-start.2
  148.6 2.6 collective-permute-done.2
  155.0 13.1 %all_to_all.53 = f32[8,8,512]{2,1,0:T(8,128)} all-to-all(f32[8,8,512]{2,1,0:T(8,128)S(1)} %broadcast_in_dim.26), channel_id=1, replica_groups=mesh['chip'=32,'core'=2,'region'=8] {'region'}, dimensions={0} | all-to-all | bytes 262144 | tf_op jit(solution)/shard_map/all_to_all | solution.py:37
  169.1 20.6 %all_to_all.54 = f32[32,8,512]{2,1,0:T(8,128)S(1)} all-to-all(f32[32,8,512]{2,1,0:T(8,128)S(1)} %broadcast_in_dim.27), channel_id=1, replica_groups=mesh['chip'=32,'core'=2,'region'=8] {'chip'}, dimensions={0} | all-to-all | bytes 1048576 | tf_op jit(solution)/shard_map/all_to_all | solution.py:37
  189.7 2.1 collective-permute-start.3
  193.7 22.0 %latent_parts.1 = f32[8,72,256]{2,1,0:T(8,128)S(1)} custom-call(f32[256,512]{1,0:T(8,128)S(1)} %get-tuple-element.22.gram_low, f32[256,512]{1,0:T(8,128)S(1)} %get-tuple-element.21.gram_high, f32[256,768]{1,0:T(8,128)S(1)} %copy-done.2, f32[256,768]{1,0:T(8,128)S(1)} %copy-done.4, f32[64,512]{1,0:T(8,128)S(1)} %bitcast.45, ...), custom_call_target="tpu_custom_call" | custom-call | flops 268435456 | bytes 8388608 | tf_op jit(solution)/shard_map/latent_parts/pallas_call | solution.py:134
  215.7 22.6 %all_to_all.55 = f32[8,72,256]{2,1,0:T(8,128)} all-to-all(f32[8,72,256]{2,1,0:T(8,128)S(1)} %latent_parts.1), channel_id=1, replica_groups=mesh['chip'=32,'core'=2,'region'=8] {'region'}, dimensions={0} | all-to-all | bytes 1179648 | tf_op jit(solution)/shard_map/all_to_all | solution.py:32
  241.8 4.2 %all-to-all-start.7 = ((f32[8,72,256]{2,1,0:T(8,128)}), f32[8,72,256]{2,1,0:T(8,128)}, u32[]{:S(2)}, u32[]{:S(2)}) async-start(f32[8,72,256]{2,1,0:T(8,128)} %broadcast_in_dim.28), calls=%async_computation.7 | async-start | bytes 1179648 | tf_op jit(solution)/shard_map/all_to_all | solution.py:37
  246.1 19.3 %all-to-all-done.7.latents = f32[8,72,256]{2,1,0:T(8,128)} async-done(((f32[8,72,256]{2,1,0:T(8,128)}), f32[8,72,256]{2,1,0:T(8,128)}, u32[]{:S(2)}, u32[]{:S(2)}) %all-to-all-start.7) | async-done | bytes 589856 | tf_op jit(solution)/shard_map/all_to_all | solution.py:37
  266.3 6.5 %error_stats.1 = (f32[64,2048]{1,0:T(8,128)}, f32[1,2048]{1,0:T(1,128)S(1)}, f32[64,8,128]{2,1,0:T(8,128)S(1)}) custom-call(f32[8,72,256]{2,1,0:T(8,128)} %all-to-all-done.7.latents, bf16[8,80,256]{2,1,0:T(8,128)(2,1)S(1)} %all-to-all-done.1.signals, bf16[768,2048]{1,0:T(8,128)(2,1)S(1)} %copy-done, bf16[768,128]{1,0:T(8,128)(2,1)S(1)} %copy-done.5, ...), custom_call_target="tpu_custom_call" | custom-call | flops 805306368 | bytes 8388608 | tf_op jit(solution)/shard_map/error_stats/pallas_call | solution.py:228
  272.8 19.2 %all_to_all.56 = f32[64,1,8,128]{3,2,1,0:T(8,128)S(1)} all-to-all(f32[64,1,8,128]{3,2,1,0:T(8,128)S(1)} %bitcast.44), channel_id=1, replica_groups=mesh['chip'=32,'core'=2,'region'=8] {'chip','core'}, dimensions={0} | all-to-all | bytes 524288 | tf_op jit(solution)/shard_map/all_to_all | solution.py:32
  292.8 6.5 %all-to-all-start.9 = ((f32[64,1,8,128]{3,2,1,0:T(8,128)}), f32[64,1,8,128]{3,2,1,0:T(8,128)S(1)}, u32[]{:S(2)}, u32[]{:S(2)}) async-start(f32[64,1,8,128]{3,2,1,0:T(8,128)} %broadcast_in_dim.29), calls=%async_computation.9 | async-start | bytes 524288 | tf_op jit(solution)/shard_map/all_to_all | solution.py:37
  299.3 15.0 %psum.7 = f32[2048]{0:T(1024)S(1)} all-reduce(f32[2048]{0:T(1024)S(1)} %bitcast.46), channel_id=1, replica_groups=mesh['chip'=32,'core'=2,'region'=8] {'region'}, use_global_device_ids=true, to_apply=%region_4.5 | all-reduce | flops 2048 | bytes 16384 | tf_op jit(solution)/shard_map/psum | solution.py:351
  (68 shorter events, 30.3 us)
Async XLA Ops:
  7.2 66.8 %all-gather.2.cloned.1.call-start = ((), (), s32[]{:S(2)}) async-start(), calls=%async_computation.10 | async-start | bytes 2359296 | tf_op jit(solution)/shard_map/all_gather | solution.py:310
  9.1 11.9 %collective-permute-start = (bf16[768]{0:T(1024)(128)(2,1)S(1)}, bf16[768]{0:T(1024)(128)(2,1)S(1)}, u32[]{:S(2)}, u32[]{:S(2)}) collective-permute-start(bf16[768]{0:T(1024)(128)(2,1)S(1)} %slice_reduce_fusion), channel_id=1, source_target_pairs={{0,8},{8,16},{16,24},{24,32},{32,40},{40,48},{48,56},{56,64},{64,7... | collective-permute-start | bytes 4616 | tf_op jit(solution)/shard_map/ppermute | solution.py:311
  11.7 3.2 copy-start.12
  16.2 43.2 %copy-start.9 = (bf16[768,8]{0,1:T(8,128)(2,1)S(1)}, bf16[768,8]{0,1:T(8,128)(2,1)}, u32[]{:S(2)}) copy-start(bf16[768,8]{0,1:T(8,128)(2,1)} %param.17) | copy-start | bytes 36868
  16.2 43.2 %copy-start.11 = (s32[8,8]{1,0:T(8,128)S(1)}, s32[8,8]{1,0:T(8,128)}, u32[]{:S(2)}) copy-start(s32[8,8]{1,0:T(8,128)} %param.19) | copy-start | bytes 772
  16.2 57.8 %copy-start = (bf16[768,2048]{1,0:T(8,128)(2,1)S(1)}, bf16[768,2048]{1,0:T(8,128)(2,1)}, u32[]{:S(2)}) copy-start(bf16[768,2048]{1,0:T(8,128)(2,1)} %activity.3) | copy-start | bytes 9437188
  56.0 18.0 %all-to-all-start.1 = ((bf16[8,80,256]{2,1,0:T(8,128)(2,1)}), bf16[8,80,256]{2,1,0:T(8,128)(2,1)S(1)}, u32[]{:S(2)}, u32[]{:S(2)}) async-start(bf16[8,80,256]{2,1,0:T(8,128)(2,1)} %broadcast_in_dim.23), calls=%async_computation.1 | async-start | bytes 655360 | tf_op jit(solution)/shard_map/all_to_all | solution.py:37
  77.1 4.5 %collective-permute-start.1 = (f32[256,768]{1,0:T(8,128)}, f32[256,768]{1,0:T(8,128)}, u32[]{:S(2)}, u32[]{:S(2)}) collective-permute-start(f32[256,768]{1,0:T(8,128)} %fusion.1), channel_id=1, source_target_pairs={{0,8},{8,0},{1,9},{9,1},{2,10},{10,2},{3,11},{11,3},{4,12},{12,4},... | collective-permute-start | bytes 2359304 | tf_op jit(solution)/shard_map/ppermute | solution.py:28
  146.7 4.5 %collective-permute-start.2 = (f32[256,768]{1,0:T(8,128)}, f32[256,768]{1,0:T(8,128)}, u32[]{:S(2)}, u32[]{:S(2)}) collective-permute-start(f32[256,768]{1,0:T(8,128)} %bitcast.11), channel_id=1, source_target_pairs={{0,8},{8,0},{1,9},{9,1},{2,10},{10,2},{3,11},{11,3},{4,12},{12,4},... | collective-permute-start | bytes 2359304 | tf_op jit(solution)/shard_map/ppermute | solution.py:28
  152.6 1.6 copy-start.3
  153.4 0.9 copy-start.1
  169.0 24.6 %copy-start.2 = (f32[256,768]{1,0:T(8,128)S(1)}, f32[256,768]{1,0:T(8,128)}, u32[]{:S(2)}) copy-start(f32[256,768]{1,0:T(8,128)} %copy-done.1) | copy-start | bytes 2359300
  169.0 24.6 %copy-start.4 = (f32[256,768]{1,0:T(8,128)S(1)}, f32[256,768]{1,0:T(8,128)}, u32[]{:S(2)}) copy-start(f32[256,768]{1,0:T(8,128)} %copy-done.3) | copy-start | bytes 2359300
  169.0 24.6 %copy-start.6 = (f32[512,64]{0,1:T(8,128)S(1)}, f32[512,64]{0,1:T(8,128)}, u32[]{:S(2)}) copy-start(f32[512,64]{0,1:T(8,128)} %param.12) | copy-start | bytes 393220
  189.7 3.8 %collective-permute-start.3 = (f32[256,512]{1,0:T(8,128)S(1)}, f32[256,512]{1,0:T(8,128)S(1)}, u32[]{:S(2)}, u32[]{:S(2)}) collective-permute-start(f32[256,512]{1,0:T(8,128)S(1)} %bitcast.48), channel_id=1, source_target_pairs={{0,8},{8,0},{1,9},{9,1},{2,10},{10,2},{3,11},{11,3},{4,12},{12,4},... | collective-permute-start | bytes 1572872 | tf_op jit(solution)/shard_map/ppermute | solution.py:28
  215.7 30.3 %copy-start.10 = (f32[64]{0:T(128)S(1)}, f32[64]{0:T(128)}, u32[]{:S(2)}) copy-start(f32[64]{0:T(128)} %param.14) | copy-start | bytes 772
  215.7 49.7 %copy-start.7 = (f32[64,64]{1,0:T(8,128)S(1)}, f32[64,64]{1,0:T(8,128)}, u32[]{:S(2)}) copy-start(f32[64,64]{1,0:T(8,128)} %recurrent.1) | copy-start | bytes 49156
  241.8 23.6 %all-to-all-start.7 = ((f32[8,72,256]{2,1,0:T(8,128)}), f32[8,72,256]{2,1,0:T(8,128)}, u32[]{:S(2)}, u32[]{:S(2)}) async-start(f32[8,72,256]{2,1,0:T(8,128)} %broadcast_in_dim.28), calls=%async_computation.7 | async-start | bytes 1179648 | tf_op jit(solution)/shard_map/all_to_all | solution.py:37
  265.4 0.9 copy-start.5
  292.8 22.0 %all-to-all-start.9 = ((f32[64,1,8,128]{3,2,1,0:T(8,128)}), f32[64,1,8,128]{3,2,1,0:T(8,128)S(1)}, u32[]{:S(2)}, u32[]{:S(2)}) async-start(f32[64,1,8,128]{3,2,1,0:T(8,128)} %broadcast_in_dim.29), calls=%async_computation.9 | async-start | bytes 524288 | tf_op jit(solution)/shard_map/all_to_all | solution.py:37
  314.8 0.7 copy-start.8
Sparse Core Ops, SparseCore 0:
  10.1 61.4 all-gather.1

commit v3 on v2

--- a/solution.py
+++ b/solution.py
@@ -29,17 +29,12 @@
 
 
 def scatter_sum(pieces, axis):
-    return jnp.sum(lax.all_to_all(pieces, axis, 0, 0), axis=0)
+    return jnp.sum(lax.all_to_all(pieces, axis, 0, 0).astype(full), axis=0)
 
 
 def share(x, axis):
     copies = jnp.broadcast_to(x[None], (lax.axis_size(axis),) + x.shape)
     return lax.all_to_all(lax.optimization_barrier(copies), axis, 0, 0)
-
-
-def in_core_order(mine, theirs):
-    first = lax.axis_index("core") == 0
-    return jnp.where(first, mine, theirs), jnp.where(first, theirs, mine)
 
 
 def inverse_factor(tile):
@@ -89,12 +84,15 @@
 
 
 def latents_kernel(
-    gram_low, gram_high, sketch_low, sketch_high, mix, before, activity, out, work, inverse, weights
+    core, gram, gram_other, sketch, sketch_other, mix, before, activity,
+    out, work, inverse, weights,
 ):
     n = work.shape[0]
     mid = n // 2
-    work[:mid, :] = gram_low[...]
-    work[mid:, :] = gram_high[...]
+    here = pl.ds(pl.multiple_of(core[0] * mid, mid), mid)
+    there = pl.ds(pl.multiple_of((1 - core[0]) * mid, mid), mid)
+    work[here, :] = gram[...]
+    work[there, :] = gram_other[...]
     starts = range(0, n, BLOCK)
     for a in starts:
         e = a + BLOCK
@@ -109,8 +107,8 @@
         if e < n:
             rest = rest - product(weights[:, e:], work[e:, a:e], 1, 0, precise)
         weights[:, a:e] = product(rest, inverse[a:e, :], 1, 0, precise)
-    loading = product(weights[:, :mid], sketch_low[...], 1, 0, precise)
-    loading = loading + product(weights[:, mid:], sketch_high[...], 1, 0, precise)
+    loading = product(weights[:, here], sketch[...], 1, 0, precise)
+    loading = loading + product(weights[:, there], sketch_other[...], 1, 0, precise)
     loading = loading.astype(half)
     rank = loading.shape[0]
     pieces, rows, width = out.shape
@@ -127,14 +125,71 @@
     return [pl.BlockSpec(memory_space=pltpu.VMEM)] * count
 
 
-def latent_parts(gram, sketch, mix, before, activity, pieces):
+def scalar():
+    return pl.BlockSpec(memory_space=pltpu.SMEM)
+
+
+def gram_kernel(core, own, sketch, sketch_other, out):
+    mid = sketch.shape[0]
+    mine = product(own[...], sketch[...], 1, 1, precise)
+    other = product(own[...], sketch_other[...], 1, 1, precise)
+    first = core[0] == 0
+    low, high = jnp.where(first, mine, other), jnp.where(first, other, mine)
+    for i in range(out.shape[0]):
+        out[i, :, :mid] = low
+        out[i, :, mid:] = high
+
+
+def gram_rows(core, own, sketch, copies):
+    rows, columns = own.shape[0], 2 * sketch[0].shape[0]
+    return pl.pallas_call(
+        gram_kernel,
+        out_shape=jax.ShapeDtypeStruct((copies, rows, columns), full),
+        in_specs=[scalar()] + in_vmem(3),
+        out_specs=in_vmem(1)[0],
+        compiler_params=pltpu.CompilerParams(vmem_limit_bytes=16 * 2**20),
+        cost_estimate=pl.CostEstimate(
+            flops=2 * rows * columns * own.shape[1], bytes_accessed=2 * 2**20, transcendentals=0
+        ),
+        name="gram_rows",
+    )(core, own, *sketch)
+
+
+def signals_kernel(feed, before, activity, out):
+    pieces, rows, width = out.shape
+    rank = feed.shape[0]
+    prior = product(before[...], feed[...], 1, 1).astype(half)
+    for i in range(pieces):
+        signal = product(feed[...], activity[:, i * width : (i + 1) * width], 1, 0)
+        out[i, :rank, :] = signal.astype(half)
+        out[i, rank:, :] = jnp.zeros((rows - rank, width), half)
+        out[i, rank:, :rank] = prior
+
+
+def signal_parts(feed, before, activity, pieces):
+    rank, neurons = feed.shape
+    frames = activity.shape[1]
+    return pl.pallas_call(
+        signals_kernel,
+        out_shape=jax.ShapeDtypeStruct((pieces, rank + before.shape[0], frames // pieces), half),
+        in_specs=in_vmem(3),
+        out_specs=in_vmem(1)[0],
+        compiler_params=pltpu.CompilerParams(vmem_limit_bytes=16 * 2**20),
+        cost_estimate=pl.CostEstimate(
+            flops=2 * rank * neurons * frames, bytes_accessed=4 * 2**20, transcendentals=0
+        ),
+        name="signal_parts",
+    )(feed, before, activity)
+
+
+def latent_parts(core, gram, sketch, mix, before, activity, pieces):
     n = mix.shape[1]
     rank = mix.shape[0]
     frames = activity.shape[1]
     return pl.pallas_call(
         latents_kernel,
         out_shape=jax.ShapeDtypeStruct((pieces, rank + 8, frames // pieces), full),
-        in_specs=in_vmem(7),
+        in_specs=[scalar()] + in_vmem(7),
         out_specs=in_vmem(1)[0],
         scratch_shapes=[
             pltpu.VMEM((n, n), full),
@@ -146,7 +201,7 @@
             flops=2 * n**3, bytes_accessed=8 * 2**20, transcendentals=n
         ),
         name="latent_parts",
-    )(*gram, *sketch, mix, before, activity)
+    )(core, *gram, *sketch, mix, before, activity)
 
 
 def lag(block, carry):
@@ -318,33 +373,41 @@
     region_feed, spread = region_tables(my_blocks, region_mask, region_in, region_out)
     maps = jnp.concatenate([readout, spread], axis=1)
     rank = region_feed.shape[1]
-    signal = product(region_feed, activity, 0, 0)
-    signal = signal.reshape(rank, regions, -1).transpose(1, 0, 2)
-    prior = product(before, region_feed, 1, 0)
-    prior = jnp.pad(prior, ((0, 0), (0, signal.shape[2] - rank)))
-    prior = jnp.broadcast_to(prior[None], (regions,) + prior.shape)
-    signal = scatter_sum(jnp.concatenate([signal, prior], axis=1), "region")
-    signals = share(signal.astype(half), "region")
+    signal = signal_parts(region_feed.T, before, activity, regions)
+    signals = share(scatter_sum(signal, "region").astype(half), "region")
+
+    largest = jnp.maximum(jnp.max(jnp.abs(basis_mix), axis=0), 1e-30)
+    width = frames_here // regions
+    unit = jnp.concatenate(
+        [
+            jnp.broadcast_to(largest[:, None], (rank, width)),
+            jnp.broadcast_to(jnp.pad(largest, (0, width - rank), constant_values=1.0), (8, width)),
+        ]
+    )
+    unit = unit / 4
     bias = latent_bias[:, None]
-    test_full, signals, maps, before, bias = lax.optimization_barrier(
-        (test_full, signals, maps, before, bias)
+    test_full, signals, maps, before, bias, unit, per_unit = lax.optimization_barrier(
+        (test_full, signals, maps, before, bias, unit, 1 / unit)
     )
 
     mid = columns // CORES
     theirs = product(lax.dynamic_slice_in_dim(test_full, (1 - core) * mid, mid), activity, 1, 1)
+    theirs = other_core(theirs)
     mine = product(lax.dynamic_slice_in_dim(test_full, core * mid, mid), activity, 1, 1)
-    mine = mine + other_core(theirs)
+    mine = lax.optimization_barrier(mine) + theirs
     own = scatter_sum(mine.reshape(chips, mid // chips, neurons_here), "chip")
     mine = share(own, "chip").reshape(mid, neurons_here)
-    sketch = in_core_order(mine, other_core(mine))
-
-    rows = jnp.concatenate([product(own, part, 1, 1, precise) for part in sketch], axis=1)
-    rows = jnp.sum(share(rows, "region"), axis=0)
+    sketch = mine, other_core(mine)
+
+    core = core.reshape(1)
+    rows = lax.all_to_all(gram_rows(core, own, sketch, regions), "region", 0, 0)
+    rows = jnp.sum(rows, axis=0)
     mine = share(rows, "chip").reshape(mid, columns)
-    gram = in_core_order(mine, other_core(mine))
-
-    parts = latent_parts(gram, sketch, basis_mix.T, before, activity, regions)
-    latents = share(scatter_sum(parts, "region"), "region")
+    gram = mine, other_core(mine)
+
+    parts = latent_parts(core, gram, sketch, basis_mix.T, before, activity, regions)
+    latents = scatter_sum((parts * per_unit).astype(jnp.float16), "region")
+    latents = share(latents.astype(jnp.float16), "region").astype(full) * unit
     latents_out, frame_sq, stats = error_stats(
         latents, signals, activity, maps, recurrent, bias
     )

time: 326 us -> 304 us (0.933)
  blocking collectives: 185 us -> 147 us
  waiting for transfers between devices: 40 us -> 47.9 us
  starting transfers between devices: 22 us -> 28.9 us
    all_to_all x4, blocking collectives: 108 us -> 83.6 us  [the longest x3 69.2 us: scatter_sum(): return jnp.sum(lax.all_to_all(pieces, axis, 0, 0).astype(full), axis=0)]
    all_to_all x0 -> x1, waiting for transfers between devices: none -> 13.3 us  [scatter_sum(): return jnp.sum(lax.all_to_all(pieces, axis, 0, 0).astype(full), axis=0)]
    all_to_all x3 -> x2, blocking collectives: 62.1 us -> 48.8 us  [share(): return lax.all_to_all(lax.optimization_barrier(copies), axis, 0, 0)]
    all_to_all x3, waiting for transfers between devices: 27.7 us -> 19.7 us  [share(): return lax.all_to_all(lax.optimization_barrier(copies), axis, 0, 0)]
    all_to_all x0 -> x1, starting transfers between devices: none -> 7.1 us  [scatter_sum(): return jnp.sum(lax.all_to_all(pieces, axis, 0, 0).astype(full), axis=0)]
    unnamed x27 -> x29, local copies, waits for them, and re-layouts: 4.3 us -> 9.31 us
    ppermute x1, waiting for transfers between devices: 4.73 us -> 8.37 us  [local(): lax.ppermute(activity[:, -1], SLAB, [(i, i + 1) for i in range(slabs - 1)])]
    dot_general x6 -> x2, matrix products: 8.21 us -> 5.37 us  [product(): lax.dot_general(a, b, (((ca,), (cb,)), ((), ())), precision=precision, pr...]
  transfers between devices with their start and end apart: 8 -> 9, of which waited for: 6 -> 8; matrix products, arithmetic and copies ran while one was open for 5% -> 5% of each run, Pallas kernels for 0% -> 0%
where the time goes in v3:
time: 304 us; the launch traced here: 302 us
  blocking collectives  147 us (48%)
  waiting for transfers between devices  47.9 us (16%)
  Pallas kernels  32.4 us (11%)
  starting transfers between devices  28.9 us (10%)
  local copies, waits for them, and re-layouts  15.4 us (5%)
  between operations  14.3 us (5%)
  other arithmetic  10.3 us (3%)
  matrix products  5.61 us (2%)
    all_to_all x3, blocking collectives, scatter_sum(): return jnp.sum(lax.all_to_all(pieces, axis, 0, 0).astype(full), axis=0)  69.2 us
    all_to_all x2, blocking collectives, share(): return lax.all_to_all(lax.optimization_barrier(copies), axis, 0, 0)  48.8 us
    pallas_call x1, Pallas kernels, latent_parts(): pl.pallas_call(latents_kernel, out_shape=jax.ShapeDtypeStruct((pieces, ra...  22.6 us
    all_to_all x3, waiting for transfers between devices, share(): return lax.all_to_all(lax.optimization_barrier(copies), axis, 0, 0)  19.7 us
    psum x1, blocking collectives, local(): frame_sq = lax.psum(frame_sq.reshape(frames_here), 'region')  15 us
    all_to_all x1, blocking collectives, local(): rows = lax.all_to_all(gram_rows(core, own, sketch, regions), 'region', 0, 0)  14.4 us
    all_to_all x3, starting transfers between devices, share(): return lax.all_to_all(lax.optimization_barrier(copies), axis, 0, 0)  14 us
    all_to_all x1, waiting for transfers between devices, scatter_sum(): return jnp.sum(lax.all_to_all(pieces, axis, 0, 0).astype(full), axis=0)  13.3 us
  transfers between devices with their start and end apart: 9, of which 8 were waited for; matrix products, arithmetic and copies ran while one was open for 5% of the time, Pallas kernels for 0%

profile of v3, /device:TPU:6, one launch (start us, length us, event | category | flops | bytes accessed | tf_op | source)
XLA Modules:
  0.0 302.3 jit_solution(8981023230196609534)
XLA Ops:
  9.1 1.9 collective-permute-start
  12.6 8.4 %collective-permute-done = bf16[768]{0:T(1024)(128)(2,1)S(1)} collective-permute-done((bf16[768]{0:T(1024)(128)(2,1)S(1)}, bf16[768]{0:T(1024)(128)(2,1)S(1)}, u32[]{:S(2)}, u32[]{:S(2)}) %collective-permute-start) | collective-permute-done | bytes 1568 | tf_op jit(solution)/shard_map/ppermute | solution.py:366
  24.2 7.1 %all-to-all-start = ((bf16[8,80,256]{2,1,0:T(8,128)(2,1)}), bf16[8,80,256]{2,1,0:T(8,128)(2,1)S(1)}, u32[]{:S(2)}, u32[]{:S(2)}) async-start(bf16[8,80,256]{2,1,0:T(8,128)(2,1)} %signal_parts.1), calls=%async_computation | async-start | bytes 655360 | tf_op jit(solution)/shard_map/all_to_all | solution.py:32
  32.2 13.3 %all-to-all-done = bf16[8,80,256]{2,1,0:T(8,128)(2,1)S(1)} async-done(((bf16[8,80,256]{2,1,0:T(8,128)(2,1)}), bf16[8,80,256]{2,1,0:T(8,128)(2,1)S(1)}, u32[]{:S(2)}, u32[]{:S(2)}) %all-to-all-start) | async-done | bytes 327712 | tf_op jit(solution)/shard_map/all_to_all | solution.py:32
  46.3 3.4 %all-to-all-start.1 = ((bf16[8,80,256]{2,1,0:T(8,128)(2,1)}), bf16[8,80,256]{2,1,0:T(8,128)(2,1)S(1)}, u32[]{:S(2)}, u32[]{:S(2)}) async-start(bf16[8,80,256]{2,1,0:T(8,128)(2,1)} %broadcast_in_dim.22), calls=%async_computation.1 | async-start | bytes 655360 | tf_op jit(solution)/shard_map/all_to_all | solution.py:37
  56.8 7.2 %all-to-all-done.1.signals = bf16[8,80,256]{2,1,0:T(8,128)(2,1)S(1)} async-done(((bf16[8,80,256]{2,1,0:T(8,128)(2,1)}), bf16[8,80,256]{2,1,0:T(8,128)(2,1)S(1)}, u32[]{:S(2)}, u32[]{:S(2)}) %all-to-all-start.1) | async-done | bytes 327712 | tf_op jit(solution)/shard_map/all_to_all | solution.py:37
  65.6 3.1 %fusion = f32[256,768]{1,0:T(8,128)} fusion(bf16[768,2048]{1,0:T(8,128)(2,1)S(1)} %copy-done.1, bf16[512,2048]{1,0:T(8,128)(2,1)} %all-gather.2.cloned.1.call-done, s32[]{:T(128)S(6)} %select_n.11), kind=kOutput, calls=%fused_computation | convolution fusion | flops 805306368 | bytes 4980740 | tf_op jit(solution)/shard_map/dot_general | solution.py:22
  68.7 1.9 collective-permute-start.1
  70.6 2.2 fusion.2
  74.5 34.3 %all_to_all.50 = f32[32,8,768]{2,1,0:T(8,128)} all-to-all(f32[32,8,768]{2,1,0:T(8,128)S(1)} %add_bitcast_fusion), channel_id=1, replica_groups=mesh['chip'=32,'core'=2,'region'=8] {'chip'}, dimensions={0} | all-to-all | bytes 1572864 | tf_op jit(solution)/shard_map/all_to_all | solution.py:32
  110.1 28.3 %all_to_all.51 = f32[32,8,768]{2,1,0:T(8,128)S(1)} all-to-all(f32[32,8,768]{2,1,0:T(8,128)S(1)} %broadcast_in_dim.26), channel_id=1, replica_groups=mesh['chip'=32,'core'=2,'region'=8] {'chip'}, dimensions={0} | all-to-all | bytes 1572864 | tf_op jit(solution)/shard_map/all_to_all | solution.py:37
  138.4 1.9 collective-permute-start.2
  140.3 2.3 collective-permute-done.2.sketch_other
  144.8 14.4 %all_to_all.52 = f32[8,8,512]{2,1,0:T(8,128)} all-to-all(f32[8,8,512]{2,1,0:T(8,128)S(1)} %gram_rows.1), channel_id=1, replica_groups=mesh['chip'=32,'core'=2,'region'=8] {'region'}, dimensions={0} | all-to-all | bytes 262144 | tf_op jit(solution)/shard_map/all_to_all | solution.py:403
  160.2 20.5 %all_to_all.53 = f32[32,8,512]{2,1,0:T(8,128)S(1)} all-to-all(f32[32,8,512]{2,1,0:T(8,128)S(1)} %broadcast_in_dim.27), channel_id=1, replica_groups=mesh['chip'=32,'core'=2,'region'=8] {'chip'}, dimensions={0} | all-to-all | bytes 1048576 | tf_op jit(solution)/shard_map/all_to_all | solution.py:37
  180.7 2.1 collective-permute-start.3
  187.7 22.6 %latent_parts.1 = f32[8,72,256]{2,1,0:T(8,128)S(1)} custom-call(s32[1]{0:T(128)} %bitcast.core, f32[256,512]{1,0:T(8,128)S(1)} %bitcast.30, f32[256,512]{1,0:T(8,128)S(1)} %collective-permute-done.3.gram_other, f32[256,768]{1,0:T(8,128)S(1)} %bitcast.28, f32[256,768]{1,0:T(8,128)S(1)} %copy-done.5, f32[64,512]{1,0:T(8,128)S(1)} %bitcast.31, ...), custom_call_target="tpu_custom_call" | custom-call | flops 268435456 | bytes 8388608 | tf_op jit(solution)/shard_map/latent_parts/pallas_call | solution.py:189
  210.3 15.5 %all_to_all.54 = f16[8,72,256]{2,1,0:T(8,128)(2,1)S(1)} all-to-all(f16[8,72,256]{2,1,0:T(8,128)(2,1)S(1)} %multiply_convert_fusion), channel_id=1, replica_groups=mesh['chip'=32,'core'=2,'region'=8] {'region'}, dimensions={0} | all-to-all | bytes 589824 | tf_op jit(solution)/shard_map/all_to_all | solution.py:32
  226.7 4.1 %all-to-all-start.7 = ((f16[8,72,256]{2,1,0:T(8,128)(2,1)}), f16[8,72,256]{2,1,0:T(8,128)(2,1)}, u32[]{:S(2)}, u32[]{:S(2)}) async-start(f16[8,72,256]{2,1,0:T(8,128)(2,1)} %broadcast_in_dim.28), calls=%async_computation.7 | async-start | bytes 589824 | tf_op jit(solution)/shard_map/all_to_all | solution.py:37
  230.8 12.5 %all-to-all-done.7 = f16[8,72,256]{2,1,0:T(8,128)(2,1)} async-done(((f16[8,72,256]{2,1,0:T(8,128)(2,1)}), f16[8,72,256]{2,1,0:T(8,128)(2,1)}, u32[]{:S(2)}, u32[]{:S(2)}) %all-to-all-start.7) | async-done | bytes 294944 | tf_op jit(solution)/shard_map/all_to_all | solution.py:37
  245.3 5.4 %error_stats.1 = (f32[64,2048]{1,0:T(8,128)}, f32[1,2048]{1,0:T(1,128)S(1)}, f32[64,8,128]{2,1,0:T(8,128)S(1)}) custom-call(f32[8,72,256]{2,1,0:T(8,128)S(1)} %convert_multiply_fusion.latents, bf16[8,80,256]{2,1,0:T(8,128)(2,1)S(1)} %all-to-all-done.1.signals, bf16[768,2048]{1,0:T(8,128)(2,1)S(1)} %copy-done.1, bf16[768,128]{1,0:T(8,128)(2,1)S(1)} %copy-done.6, ...), custom_call_target="tpu_custom_call" | custom-call | flops 805306368 | bytes 8388608 | tf_op jit(solution)/shard_map/error_stats/pallas_call | solution.py:283
  250.7 19.3 %all_to_all.55 = f32[64,1,8,128]{3,2,1,0:T(8,128)S(1)} all-to-all(f32[64,1,8,128]{3,2,1,0:T(8,128)S(1)} %bitcast.32), channel_id=1, replica_groups=mesh['chip'=32,'core'=2,'region'=8] {'chip','core'}, dimensions={0} | all-to-all | bytes 524288 | tf_op jit(solution)/shard_map/all_to_all | solution.py:32
  270.9 6.5 %all-to-all-start.9 = ((f32[64,1,8,128]{3,2,1,0:T(8,128)}), f32[64,1,8,128]{3,2,1,0:T(8,128)S(1)}, u32[]{:S(2)}, u32[]{:S(2)}) async-start(f32[64,1,8,128]{3,2,1,0:T(8,128)} %broadcast_in_dim.29), calls=%async_computation.9 | async-start | bytes 524288 | tf_op jit(solution)/shard_map/all_to_all | solution.py:37
  277.3 15.0 %psum.7 = f32[2048]{0:T(1024)S(1)} all-reduce(f32[2048]{0:T(1024)S(1)} %bitcast.33), channel_id=1, replica_groups=mesh['chip'=32,'core'=2,'region'=8] {'region'}, use_global_device_ids=true, to_apply=%region_5.6 | all-reduce | flops 2048 | bytes 16384 | tf_op jit(solution)/shard_map/psum | solution.py:414
  (72 shorter events, 34.7 us)
Async XLA Ops:
  7.2 24.1 %copy-start.11 = (bf16[768,8]{0,1:T(8,128)(2,1)S(1)}, bf16[768,8]{0,1:T(8,128)(2,1)}, u32[]{:S(2)}) copy-start(bf16[768,8]{0,1:T(8,128)(2,1)} %param.17) | copy-start | bytes 36868
  7.2 24.1 %copy-start.13 = (s32[8,8]{1,0:T(8,128)S(1)}, s32[8,8]{1,0:T(8,128)}, u32[]{:S(2)}) copy-start(s32[8,8]{1,0:T(8,128)} %param.19) | copy-start | bytes 772
  7.2 58.4 %all-gather.2.cloned.1.call-start = ((), (), s32[]{:S(2)}) async-start(), calls=%async_computation.10 | async-start | bytes 2359296 | tf_op jit(solution)/shard_map/all_gather | solution.py:365
  9.1 11.9 %collective-permute-start = (bf16[768]{0:T(1024)(128)(2,1)S(1)}, bf16[768]{0:T(1024)(128)(2,1)S(1)}, u32[]{:S(2)}, u32[]{:S(2)}) collective-permute-start(bf16[768]{0:T(1024)(128)(2,1)S(1)} %slice_reduce_fusion), channel_id=1, source_target_pairs={{0,8},{8,16},{16,24},{24,32},{32,40},{40,48},{48,56},{56,64},{64,7... | collective-permute-start | bytes 4616 | tf_op jit(solution)/shard_map/ppermute | solution.py:366
  21.0 1.9 copy-start
  22.9 42.7 %copy-start.1 = (bf16[768,2048]{1,0:T(8,128)(2,1)S(1)}, bf16[768,2048]{1,0:T(8,128)(2,1)}, u32[]{:S(2)}) copy-start(bf16[768,2048]{1,0:T(8,128)(2,1)} %activity.5) | copy-start | bytes 9437188
  24.2 21.3 %all-to-all-start = ((bf16[8,80,256]{2,1,0:T(8,128)(2,1)}), bf16[8,80,256]{2,1,0:T(8,128)(2,1)S(1)}, u32[]{:S(2)}, u32[]{:S(2)}) async-start(bf16[8,80,256]{2,1,0:T(8,128)(2,1)} %signal_parts.1), calls=%async_computation | async-start | bytes 655360 | tf_op jit(solution)/shard_map/all_to_all | solution.py:32
  46.3 17.7 %all-to-all-start.1 = ((bf16[8,80,256]{2,1,0:T(8,128)(2,1)}), bf16[8,80,256]{2,1,0:T(8,128)(2,1)S(1)}, u32[]{:S(2)}, u32[]{:S(2)}) async-start(bf16[8,80,256]{2,1,0:T(8,128)(2,1)} %broadcast_in_dim.22), calls=%async_computation.1 | async-start | bytes 655360 | tf_op jit(solution)/shard_map/all_to_all | solution.py:37
  68.7 4.5 %collective-permute-start.1 = (f32[256,768]{1,0:T(8,128)}, f32[256,768]{1,0:T(8,128)}, u32[]{:S(2)}, u32[]{:S(2)}) collective-permute-start(f32[256,768]{1,0:T(8,128)} %fusion), channel_id=1, source_target_pairs={{0,8},{8,0},{1,9},{9,1},{2,10},{10,2},{3,11},{11,3},{4,12},{12,4},... | collective-permute-start | bytes 2359304 | tf_op jit(solution)/shard_map/ppermute | solution.py:28
  138.4 4.2 %collective-permute-start.2 = (f32[256,768]{1,0:T(8,128)S(1)}, f32[256,768]{1,0:T(8,128)S(1)}, u32[]{:S(2)}, u32[]{:S(2)}) collective-permute-start(f32[256,768]{1,0:T(8,128)S(1)} %bitcast.26), channel_id=1, source_target_pairs={{0,8},{8,0},{1,9},{9,1},{2,10},{10,2},{3,11},{11,3},{4,12},{12,4},... | collective-permute-start | bytes 2359304 | tf_op jit(solution)/shard_map/ppermute | solution.py:28
  142.5 1.4 copy-start.4
  143.9 0.9 copy-start.2
  180.7 3.8 %collective-permute-start.3 = (f32[256,512]{1,0:T(8,128)S(1)}, f32[256,512]{1,0:T(8,128)S(1)}, u32[]{:S(2)}, u32[]{:S(2)}) collective-permute-start(f32[256,512]{1,0:T(8,128)S(1)} %bitcast.29), channel_id=1, source_target_pairs={{0,8},{8,0},{1,9},{9,1},{2,10},{10,2},{3,11},{11,3},{4,12},{12,4},... | collective-permute-start | bytes 1572872 | tf_op jit(solution)/shard_map/ppermute | solution.py:28
  184.5 1.1 copy-start.3
  185.6 1.1 copy-start.5
  186.8 0.9 copy-start.7
  187.7 22.6 %copy-start.10 = (f32[72,256]{1,0:T(8,128)S(1)}, f32[72,256]{1,0:T(8,128)}, u32[]{:S(2)}) copy-start(f32[72,256]{1,0:T(8,128)} %get-tuple-element.15) | copy-start | bytes 221188
  187.7 43.1 %copy-start.12 = (f32[64]{0:T(128)S(1)}, f32[64]{0:T(128)}, u32[]{:S(2)}) copy-start(f32[64]{0:T(128)} %param.14) | copy-start | bytes 772
  210.3 34.1 %copy-start.8 = (f32[64,64]{1,0:T(8,128)S(1)}, f32[64,64]{1,0:T(8,128)}, u32[]{:S(2)}) copy-start(f32[64,64]{1,0:T(8,128)} %recurrent.1) | copy-start | bytes 49156
  226.7 16.7 %all-to-all-start.7 = ((f16[8,72,256]{2,1,0:T(8,128)(2,1)}), f16[8,72,256]{2,1,0:T(8,128)(2,1)}, u32[]{:S(2)}, u32[]{:S(2)}) async-start(f16[8,72,256]{2,1,0:T(8,128)(2,1)} %broadcast_in_dim.28), calls=%async_computation.7 | async-start | bytes 589824 | tf_op jit(solution)/shard_map/all_to_all | solution.py:37
  244.4 0.9 copy-start.6
  270.9 22.1 %all-to-all-start.9 = ((f32[64,1,8,128]{3,2,1,0:T(8,128)}), f32[64,1,8,128]{3,2,1,0:T(8,128)S(1)}, u32[]{:S(2)}, u32[]{:S(2)}) async-start(f32[64,1,8,128]{3,2,1,0:T(8,128)} %broadcast_in_dim.29), calls=%async_computation.9 | async-start | bytes 524288 | tf_op jit(solution)/shard_map/all_to_all | solution.py:37
  292.9 0.7 copy-start.9
Sparse Core Ops, SparseCore 0:
  10.1 55.4 all-gather.1

commit v4 on v3

--- a/solution.py
+++ b/solution.py
@@ -83,10 +83,25 @@
     return jnp.concatenate(right, axis=0)
 
 
+def fetch(sources, targets, arrived):
+    copies = [
+        pltpu.make_async_copy(source, target, arrived.at[i])
+        for i, (source, target) in enumerate(zip(sources, targets))
+    ]
+    for copy in copies:
+        copy.start()
+    return copies
+
+
 def latents_kernel(
-    core, gram, gram_other, sketch, sketch_other, mix, before, activity,
-    out, work, inverse, weights,
+    core, gram, gram_other, before, sketch, sketch_other, mix, activity,
+    out, work, inverse, weights, sketch_here, mix_here, activity_here, arrived,
 ):
+    copies = fetch(
+        (sketch, sketch_other, mix, activity),
+        (sketch_here.at[0], sketch_here.at[1], mix_here, activity_here),
+        arrived,
+    )
     n = work.shape[0]
     mid = n // 2
     here = pl.ds(pl.multiple_of(core[0] * mid, mid), mid)
@@ -94,28 +109,40 @@
     work[here, :] = gram[...]
     work[there, :] = gram_other[...]
     starts = range(0, n, BLOCK)
+    diagonal = work[:BLOCK, :BLOCK]
     for a in starts:
         e = a + BLOCK
-        inverse[a:e, :] = inverse_factor(work[a:e, a:e])
+        factor = inverse_factor(diagonal)
+        inverse[a:e, :] = factor
         if e < n:
-            below = product(work[e:, a:e], inverse[a:e, :], 1, 1, precise)
-            work[e:, a:e] = below
-            work[e:, e:] = work[e:, e:] - product(below, below, 1, 1, precise)
+            z = e + BLOCK
+            near = product(work[e:z, a:e], factor, 1, 1, precise)
+            diagonal = work[e:z, e:z] - product(near, near, 1, 1, precise)
+            work[e:z, a:e] = near
+        if e < n and z < n:
+            far = product(work[z:, a:e], factor, 1, 1, precise)
+            work[z:, a:e] = far
+            work[z:, e:z] = work[z:, e:z] - product(far, near, 1, 1, precise)
+            work[z:, z:] = work[z:, z:] - product(far, far, 1, 1, precise)
+    copies[2].wait()
     for a in reversed(starts):
         e = a + BLOCK
-        rest = mix[:, a:e]
+        rest = mix_here[:, a:e]
         if e < n:
             rest = rest - product(weights[:, e:], work[e:, a:e], 1, 0, precise)
         weights[:, a:e] = product(rest, inverse[a:e, :], 1, 0, precise)
-    loading = product(weights[:, here], sketch[...], 1, 0, precise)
-    loading = loading + product(weights[:, there], sketch_other[...], 1, 0, precise)
+    copies[0].wait()
+    copies[1].wait()
+    loading = product(weights[:, here], sketch_here[0], 1, 0, precise)
+    loading = loading + product(weights[:, there], sketch_here[1], 1, 0, precise)
     loading = loading.astype(half)
     rank = loading.shape[0]
     pieces, rows, width = out.shape
     prior = product(before[...], loading, 1, 1)
+    copies[3].wait()
     for i in range(pieces):
         out[i, :rank, :] = product(
-            loading, activity[:, i * width : (i + 1) * width], 1, 0
+            loading, activity_here[:, i * width : (i + 1) * width], 1, 0
         )
         out[i, rank:, :] = jnp.zeros((rows - rank, width), full)
         out[i, rank:, :rank] = prior[: rows - rank, :]
@@ -123,6 +150,10 @@
 
 def in_vmem(count):
     return [pl.BlockSpec(memory_space=pltpu.VMEM)] * count
+
+
+def anywhere(count):
+    return [pl.BlockSpec(memory_space=pl.ANY)] * count
 
 
 def scalar():
@@ -189,19 +220,23 @@
     return pl.pallas_call(
         latents_kernel,
         out_shape=jax.ShapeDtypeStruct((pieces, rank + 8, frames // pieces), full),
-        in_specs=[scalar()] + in_vmem(7),
+        in_specs=[scalar()] + in_vmem(3) + anywhere(4),
         out_specs=in_vmem(1)[0],
         scratch_shapes=[
             pltpu.VMEM((n, n), full),
             pltpu.VMEM((n, BLOCK), full),
             pltpu.VMEM((rank, n), full),
+            pltpu.VMEM((2,) + sketch[0].shape, full),
+            pltpu.VMEM((rank, n), full),
+            pltpu.VMEM(activity.shape, half),
+            pltpu.SemaphoreType.DMA((4,)),
         ],
-        compiler_params=pltpu.CompilerParams(vmem_limit_bytes=40 * 2**20),
+        compiler_params=pltpu.CompilerParams(vmem_limit_bytes=58 * 2**20),
         cost_estimate=pl.CostEstimate(
             flops=2 * n**3, bytes_accessed=8 * 2**20, transcendentals=n
         ),
         name="latent_parts",
-    )(core, *gram, *sketch, mix, before, activity)
+    )(core, *gram, before, *sketch, mix, activity)
 
 
 def lag(block, carry):
@@ -223,8 +258,9 @@
 
 def error_kernel(
     latents, signals, activity, maps, recurrent, bias,
-    latents_out, frame_out, stats, cross, cross_low, squares,
+    latents_out, frame_out, stats, cross, cross_low, squares, maps_here, arrived,
 ):
+    copies = fetch((maps,), (maps_here,), arrived)
     pieces, _, width = latents.shape
     rank = recurrent.shape[0]
     neurons = activity.shape[0]
@@ -245,7 +281,9 @@
         high, low = split(hidden)
         state = jnp.concatenate([high, lagged_signal.astype(half)], axis=0)
         both = jnp.concatenate([high, low], axis=0)
-        error = activity[:, frames].astype(full) - product(maps[...], state, 1, 0)
+        if not i:
+            copies[0].wait()
+        error = activity[:, frames].astype(full) - product(maps_here[...], state, 1, 0)
         error_high, error_low = split(error)
         by_both = product(error_high, both, 1, 1)
         by_high = product(error_low, high, 1, 1)
@@ -287,12 +325,14 @@
             jax.ShapeDtypeStruct((1, frames), full),
             jax.ShapeDtypeStruct((rank, neurons // BLOCK + 2, BLOCK), full),
         ),
-        in_specs=in_vmem(6),
+        in_specs=in_vmem(3) + anywhere(1) + in_vmem(2),
         out_specs=tuple(in_vmem(3)),
         scratch_shapes=[
             pltpu.VMEM((neurons, 2 * rank), full),
             pltpu.VMEM((neurons, rank), full),
             pltpu.VMEM((neurons, BLOCK), full),
+            pltpu.VMEM(maps.shape, half),
+            pltpu.SemaphoreType.DMA((1,)),
         ],
         compiler_params=pltpu.CompilerParams(vmem_limit_bytes=40 * 2**20),
         cost_estimate=pl.CostEstimate(
@@ -374,7 +414,7 @@
     maps = jnp.concatenate([readout, spread], axis=1)
     rank = region_feed.shape[1]
     signal = signal_parts(region_feed.T, before, activity, regions)
-    signals = share(scatter_sum(signal, "region").astype(half), "region")
+    signal = scatter_sum(signal, "region").astype(half)
 
     largest = jnp.maximum(jnp.max(jnp.abs(basis_mix), axis=0), 1e-30)
     width = frames_here // regions
@@ -386,8 +426,8 @@
     )
     unit = unit / 4
     bias = latent_bias[:, None]
-    test_full, signals, maps, before, bias, unit, per_unit = lax.optimization_barrier(
-        (test_full, signals, maps, before, bias, unit, 1 / unit)
+    test_full, signal, maps, before, bias, unit, per_unit = lax.optimization_barrier(
+        (test_full, signal, maps, before, bias, unit, 1 / unit)
     )
 
     mid = columns // CORES
@@ -405,7 +445,10 @@
     mine = share(rows, "chip").reshape(mid, columns)
     gram = mine, other_core(mine)
 
+    gram, signal = lax.optimization_barrier((gram, signal))
+    signals = share(signal, "region")
     parts = latent_parts(core, gram, sketch, basis_mix.T, before, activity, regions)
+    parts, signals = lax.optimization_barrier((parts, signals))
     latents = scatter_sum((parts * per_unit).astype(jnp.float16), "region")
     latents = share(latents.astype(jnp.float16), "region").astype(full) * unit
     latents_out, frame_sq, stats = error_stats(

time: 304 us -> 302 us (level)
  local copies, waits for them, and re-layouts: 15.4 us -> 11.4 us
    all_gather x1, waiting for transfers between devices: 1.57 us -> 16 us  [local(): test_full = lax.all_gather(test_matrix.T, 'region', axis=0, tiled=True)]
    all_to_all x3, waiting for transfers between devices: 19.7 us -> 10.8 us  [share(): return lax.all_to_all(lax.optimization_barrier(copies), axis, 0, 0)]
    all_to_all x1, waiting for transfers between devices: 13.3 us -> 8.61 us  [scatter_sum(): return jnp.sum(lax.all_to_all(pieces, axis, 0, 0).astype(full), axis=0)]
    unnamed x29 -> x25, local copies, waits for them, and re-layouts: 9.31 us -> 5.27 us
  transfers between devices with their start and end apart: 9 -> 9, of which waited for: 8 -> 7; matrix products, arithmetic and copies ran while one was open for 5% -> 5% of each run, Pallas kernels for 0% -> 9%
where the time goes in v4:
time: 302 us; the launch traced here: 301 us
  blocking collectives  148 us (49%)
  waiting for transfers between devices  46.7 us (15%)
  Pallas kernels  35.3 us (12%)
  starting transfers between devices  28.9 us (10%)
  between operations  14.3 us (5%)
  local copies, waits for them, and re-layouts  11.4 us (4%)
  other arithmetic  10.1 us (3%)
  matrix products  6.3 us (2%)
    all_to_all x3, blocking collectives, scatter_sum(): return jnp.sum(lax.all_to_all(pieces, axis, 0, 0).astype(full), axis=0)  71.1 us
    all_to_all x2, blocking collectives, share(): return lax.all_to_all(lax.optimization_barrier(copies), axis, 0, 0)  48.8 us
    pallas_call x1, Pallas kernels, latent_parts(): pl.pallas_call(latents_kernel, out_shape=jax.ShapeDtypeStruct((pieces, ra...  25 us
    all_gather x1, waiting for transfers between devices, local(): test_full = lax.all_gather(test_matrix.T, 'region', axis=0, tiled=True)  16 us
    psum x1, blocking collectives, local(): frame_sq = lax.psum(frame_sq.reshape(frames_here), 'region')  15 us
    all_to_all x3, starting transfers between devices, share(): return lax.all_to_all(lax.optimization_barrier(copies), axis, 0, 0)  14.1 us
    all_to_all x1, blocking collectives, local(): rows = lax.all_to_all(gram_rows(core, own, sketch, regions), 'region', 0, 0)  12.8 us
    all_to_all x3, waiting for transfers between devices, share(): return lax.all_to_all(lax.optimization_barrier(copies), axis, 0, 0)  10.8 us
  transfers between devices with their start and end apart: 9, of which 7 were waited for; matrix products, arithmetic and copies ran while one was open for 5% of the time, Pallas kernels for 9%

profile of v4, /device:TPU:6, one launch (start us, length us, event | category | flops | bytes accessed | tf_op | source)
XLA Modules:
  0.0 300.8 jit_solution(4906697040268777264)
XLA Ops:
  9.1 1.9 collective-permute-start
  14.9 6.1 %collective-permute-done = bf16[768]{0:T(1024)(128)(2,1)S(1)} collective-permute-done((bf16[768]{0:T(1024)(128)(2,1)S(1)}, bf16[768]{0:T(1024)(128)(2,1)S(1)}, u32[]{:S(2)}, u32[]{:S(2)}) %collective-permute-start) | collective-permute-done | bytes 1568 | tf_op jit(solution)/shard_map/ppermute | solution.py:406
  24.2 7.1 %all-to-all-start = ((bf16[8,80,256]{2,1,0:T(8,128)(2,1)}), bf16[8,80,256]{2,1,0:T(8,128)(2,1)S(1)}, u32[]{:S(2)}, u32[]{:S(2)}) async-start(bf16[8,80,256]{2,1,0:T(8,128)(2,1)} %signal_parts.1), calls=%async_computation | async-start | bytes 655360 | tf_op jit(solution)/shard_map/all_to_all | solution.py:32
  38.3 8.6 %all-to-all-done = bf16[8,80,256]{2,1,0:T(8,128)(2,1)S(1)} async-done(((bf16[8,80,256]{2,1,0:T(8,128)(2,1)}), bf16[8,80,256]{2,1,0:T(8,128)(2,1)S(1)}, u32[]{:S(2)}, u32[]{:S(2)}) %all-to-all-start) | async-done | bytes 327712 | tf_op jit(solution)/shard_map/all_to_all | solution.py:32
  47.0 16.0 %all-gather.2.cloned.1.call-done = bf16[512,2048]{1,0:T(8,128)(2,1)} async-done(((bf16[64,2048]{1,0:T(8,128)(2,1)}), bf16[512,2048]{1,0:T(8,128)(2,1)}) %all-gather.2.cloned.1.call-update) | async-done | bytes 2097168 | tf_op jit(solution)/shard_map/all_gather | solution.py:405
  63.0 3.1 %fusion = f32[256,768]{1,0:T(8,128)} fusion(bf16[768,2048]{1,0:T(8,128)(2,1)S(1)} %copy-done.1, bf16[512,2048]{1,0:T(8,128)(2,1)} %all-gather.2.cloned.1.call-done, s32[]{:T(128)S(6)} %select_n.11), kind=kOutput, calls=%fused_computation | convolution fusion | flops 805306368 | bytes 4980740 | tf_op jit(solution)/shard_map/dot_general | solution.py:22
  66.2 1.9 collective-permute-start.1
  68.1 2.2 fusion.2
  71.9 32.5 %all_to_all.50 = f32[32,8,768]{2,1,0:T(8,128)S(1)} all-to-all(f32[32,8,768]{2,1,0:T(8,128)S(1)} %add_bitcast_fusion), channel_id=1, replica_groups=mesh['chip'=32,'core'=2,'region'=8] {'chip'}, dimensions={0} | all-to-all | bytes 1572864 | tf_op jit(solution)/shard_map/all_to_all | solution.py:32
  104.6 28.3 %all_to_all.51 = f32[32,8,768]{2,1,0:T(8,128)S(1)} all-to-all(f32[32,8,768]{2,1,0:T(8,128)S(1)} %broadcast_in_dim.25), channel_id=1, replica_groups=mesh['chip'=32,'core'=2,'region'=8] {'chip'}, dimensions={0} | all-to-all | bytes 1572864 | tf_op jit(solution)/shard_map/all_to_all | solution.py:37
  132.9 1.9 collective-permute-start.2
  134.8 2.3 collective-permute-done.2.sketch_other
  138.4 12.8 %all_to_all.52 = f32[8,8,512]{2,1,0:T(8,128)S(1)} all-to-all(f32[8,8,512]{2,1,0:T(8,128)S(1)} %gram_rows.1), channel_id=1, replica_groups=mesh['chip'=32,'core'=2,'region'=8] {'region'}, dimensions={0} | all-to-all | bytes 262144 | tf_op jit(solution)/shard_map/all_to_all | solution.py:443
  151.3 20.5 %all_to_all.53 = f32[32,8,512]{2,1,0:T(8,128)S(1)} all-to-all(f32[32,8,512]{2,1,0:T(8,128)S(1)} %broadcast_in_dim.26), channel_id=1, replica_groups=mesh['chip'=32,'core'=2,'region'=8] {'chip'}, dimensions={0} | all-to-all | bytes 1048576 | tf_op jit(solution)/shard_map/all_to_all | solution.py:37
  171.8 1.9 collective-permute-start.3
  176.4 3.6 %all-to-all-start.5 = ((bf16[8,80,256]{2,1,0:T(8,128)(2,1)}), bf16[8,80,256]{2,1,0:T(8,128)(2,1)S(1)}, u32[]{:S(2)}, u32[]{:S(2)}) async-start(bf16[8,80,256]{2,1,0:T(8,128)(2,1)} %broadcast_in_dim.27), calls=%async_computation.5 | async-start | bytes 655360 | tf_op jit(solution)/shard_map/all_to_all | solution.py:37
  180.1 25.0 %latent_parts.1 = f32[8,72,256]{2,1,0:T(8,128)} custom-call(s32[1]{0:T(128)} %bitcast.core, f32[256,512]{1,0:T(8,128)} %bitcast.32, f32[256,512]{1,0:T(8,128)} %copy-done.10, bf16[16,768]{1,0:T(8,128)(2,1)} %copy-done.6, f32[256,768]{1,0:T(8,128)} %bitcast.28, f32[256,768]{1,0:T(8,128)} %copy-done.4, f32[64,512]{1,0:T(8,128)} %bitcast.34, ...), custom_call_target="tpu_custom_call" | custom-call | flops 268435456 | bytes 8388608 | tf_op jit(solution)/shard_map/latent_parts/pallas_call | solution.py:220
  206.4 19.3 %all_to_all.54 = f16[8,72,256]{2,1,0:T(8,128)(2,1)S(1)} all-to-all(f16[8,72,256]{2,1,0:T(8,128)(2,1)S(1)} %multiply_convert_fusion), channel_id=1, replica_groups=mesh['chip'=32,'core'=2,'region'=8] {'region'}, dimensions={0} | all-to-all | bytes 589824 | tf_op jit(solution)/shard_map/all_to_all | solution.py:32
  226.6 4.1 %all-to-all-start.7 = ((f16[8,72,256]{2,1,0:T(8,128)(2,1)}), f16[8,72,256]{2,1,0:T(8,128)(2,1)}, u32[]{:S(2)}, u32[]{:S(2)}) async-start(f16[8,72,256]{2,1,0:T(8,128)(2,1)} %broadcast_in_dim.28), calls=%async_computation.7 | async-start | bytes 589824 | tf_op jit(solution)/shard_map/all_to_all | solution.py:37
  230.7 10.8 %all-to-all-done.7 = f16[8,72,256]{2,1,0:T(8,128)(2,1)} async-done(((f16[8,72,256]{2,1,0:T(8,128)(2,1)}), f16[8,72,256]{2,1,0:T(8,128)(2,1)}, u32[]{:S(2)}, u32[]{:S(2)}) %all-to-all-start.7) | async-done | bytes 294944 | tf_op jit(solution)/shard_map/all_to_all | solution.py:37
  243.5 5.8 %error_stats.1 = (f32[64,2048]{1,0:T(8,128)}, f32[1,2048]{1,0:T(1,128)S(1)}, f32[64,8,128]{2,1,0:T(8,128)S(1)}) custom-call(f32[8,72,256]{2,1,0:T(8,128)S(1)} %convert_multiply_fusion.latents, bf16[8,80,256]{2,1,0:T(8,128)(2,1)S(1)} %all-to-all-done.5.signals, bf16[768,2048]{1,0:T(8,128)(2,1)S(1)} %copy-done.2, bf16[768,128]{1,0:T(8,128)(2,1)S(1)} %copy-done.5, ...), custom_call_target="tpu_custom_call" | custom-call | flops 805306368 | bytes 8388608 | tf_op jit(solution)/shard_map/error_stats/pallas_call | solution.py:321
  249.3 19.2 %all_to_all.55 = f32[64,1,8,128]{3,2,1,0:T(8,128)S(1)} all-to-all(f32[64,1,8,128]{3,2,1,0:T(8,128)S(1)} %bitcast.29), channel_id=1, replica_groups=mesh['chip'=32,'core'=2,'region'=8] {'chip','core'}, dimensions={0} | all-to-all | bytes 524288 | tf_op jit(solution)/shard_map/all_to_all | solution.py:32
  269.3 6.5 %all-to-all-start.9 = ((f32[64,1,8,128]{3,2,1,0:T(8,128)}), f32[64,1,8,128]{3,2,1,0:T(8,128)S(1)}, u32[]{:S(2)}, u32[]{:S(2)}) async-start(f32[64,1,8,128]{3,2,1,0:T(8,128)} %broadcast_in_dim.29), calls=%async_computation.9 | async-start | bytes 524288 | tf_op jit(solution)/shard_map/all_to_all | solution.py:37
  275.8 15.0 %psum.7 = f32[2048]{0:T(1024)S(1)} all-reduce(f32[2048]{0:T(1024)S(1)} %bitcast.30), channel_id=1, replica_groups=mesh['chip'=32,'core'=2,'region'=8] {'region'}, use_global_device_ids=true, to_apply=%region_5.6 | all-reduce | flops 2048 | bytes 16384 | tf_op jit(solution)/shard_map/psum | solution.py:457
  (68 shorter events, 29.9 us)
Async XLA Ops:
  7.2 55.9 %all-gather.2.cloned.1.call-start = ((), (), s32[]{:S(2)}) async-start(), calls=%async_computation.10 | async-start | bytes 2359296 | tf_op jit(solution)/shard_map/all_gather | solution.py:405
  9.1 11.9 %collective-permute-start = (bf16[768]{0:T(1024)(128)(2,1)S(1)}, bf16[768]{0:T(1024)(128)(2,1)S(1)}, u32[]{:S(2)}, u32[]{:S(2)}) collective-permute-start(bf16[768]{0:T(1024)(128)(2,1)S(1)} %slice_reduce_fusion), channel_id=1, source_target_pairs={{0,8},{8,16},{16,24},{24,32},{32,40},{40,48},{48,56},{56,64},{64,7... | collective-permute-start | bytes 4616 | tf_op jit(solution)/shard_map/ppermute | solution.py:406
  21.0 1.9 copy-start
  22.9 43.3 %copy-start.6 = (bf16[16,768]{1,0:T(8,128)(2,1)}, bf16[16,768]{1,0:T(8,128)(2,1)S(1)}, u32[]{:S(2)}) copy-start(bf16[16,768]{1,0:T(8,128)(2,1)S(1)} %broadcast_in_dim.21.before) | copy-start | bytes 73732
  22.9 40.2 %copy-start.1 = (bf16[768,2048]{1,0:T(8,128)(2,1)S(1)}, bf16[768,2048]{1,0:T(8,128)(2,1)}, u32[]{:S(2)}) copy-start(bf16[768,2048]{1,0:T(8,128)(2,1)} %activity.5) | copy-start | bytes 9437188
  24.2 22.8 %all-to-all-start = ((bf16[8,80,256]{2,1,0:T(8,128)(2,1)}), bf16[8,80,256]{2,1,0:T(8,128)(2,1)S(1)}, u32[]{:S(2)}, u32[]{:S(2)}) async-start(bf16[8,80,256]{2,1,0:T(8,128)(2,1)} %signal_parts.1), calls=%async_computation | async-start | bytes 655360 | tf_op jit(solution)/shard_map/all_to_all | solution.py:32
  66.2 4.5 %collective-permute-start.1 = (f32[256,768]{1,0:T(8,128)}, f32[256,768]{1,0:T(8,128)}, u32[]{:S(2)}, u32[]{:S(2)}) collective-permute-start(f32[256,768]{1,0:T(8,128)} %fusion), channel_id=1, source_target_pairs={{0,8},{8,0},{1,9},{9,1},{2,10},{10,2},{3,11},{11,3},{4,12},{12,4},... | collective-permute-start | bytes 2359304 | tf_op jit(solution)/shard_map/ppermute | solution.py:28
  132.9 47.1 %copy-start.3 = (f32[32,8,768]{2,1,0:T(8,128)}, f32[32,8,768]{2,1,0:T(8,128)S(1)}, u32[]{:S(2)}) copy-start(f32[32,8,768]{2,1,0:T(8,128)S(1)} %all_to_all.51) | copy-start | bytes 2359300
  132.9 4.2 %collective-permute-start.2 = (f32[256,768]{1,0:T(8,128)S(1)}, f32[256,768]{1,0:T(8,128)S(1)}, u32[]{:S(2)}, u32[]{:S(2)}) collective-permute-start(f32[256,768]{1,0:T(8,128)S(1)} %bitcast.26), channel_id=1, source_target_pairs={{0,8},{8,0},{1,9},{9,1},{2,10},{10,2},{3,11},{11,3},{4,12},{12,4},... | collective-permute-start | bytes 2359304 | tf_op jit(solution)/shard_map/ppermute | solution.py:28
  137.1 43.0 %copy-start.4 = (f32[256,768]{1,0:T(8,128)}, f32[256,768]{1,0:T(8,128)S(1)}, u32[]{:S(2)}) copy-start(f32[256,768]{1,0:T(8,128)S(1)} %collective-permute-done.2.sketch_other) | copy-start | bytes 2359300
  171.8 8.2 %copy-start.8 = (f32[32,8,512]{2,1,0:T(8,128)}, f32[32,8,512]{2,1,0:T(8,128)S(1)}, u32[]{:S(2)}) copy-start(f32[32,8,512]{2,1,0:T(8,128)S(1)} %all_to_all.53) | copy-start | bytes 1572868
  171.8 3.8 %collective-permute-start.3 = (f32[256,512]{1,0:T(8,128)S(1)}, f32[256,512]{1,0:T(8,128)S(1)}, u32[]{:S(2)}, u32[]{:S(2)}) collective-permute-start(f32[256,512]{1,0:T(8,128)S(1)} %bitcast.31), channel_id=1, source_target_pairs={{0,8},{8,0},{1,9},{9,1},{2,10},{10,2},{3,11},{11,3},{4,12},{12,4},... | collective-permute-start | bytes 1572872 | tf_op jit(solution)/shard_map/ppermute | solution.py:28
  175.6 4.5 %copy-start.10 = (f32[256,512]{1,0:T(8,128)}, f32[256,512]{1,0:T(8,128)S(1)}, u32[]{:S(2)}) copy-start(f32[256,512]{1,0:T(8,128)S(1)} %collective-permute-done.3.gram_other) | copy-start | bytes 1572868
  176.4 28.7 %all-to-all-start.5 = ((bf16[8,80,256]{2,1,0:T(8,128)(2,1)}), bf16[8,80,256]{2,1,0:T(8,128)(2,1)S(1)}, u32[]{:S(2)}, u32[]{:S(2)}) async-start(bf16[8,80,256]{2,1,0:T(8,128)(2,1)} %broadcast_in_dim.27), calls=%async_computation.5 | async-start | bytes 655360 | tf_op jit(solution)/shard_map/all_to_all | solution.py:37
  180.1 50.6 %copy-start.11 = (f32[64]{0:T(128)S(1)}, f32[64]{0:T(128)}, u32[]{:S(2)}) copy-start(f32[64]{0:T(128)} %param.14) | copy-start | bytes 772
  205.1 37.5 %copy-start.2 = (bf16[768,2048]{1,0:T(8,128)(2,1)S(1)}, bf16[768,2048]{1,0:T(8,128)(2,1)}, u32[]{:S(2)}) copy-start(bf16[768,2048]{1,0:T(8,128)(2,1)} %activity.5) | copy-start | bytes 9437188
  205.1 37.5 %copy-start.7 = (f32[64,64]{1,0:T(8,128)S(1)}, f32[64,64]{1,0:T(8,128)}, u32[]{:S(2)}) copy-start(f32[64,64]{1,0:T(8,128)} %recurrent.1) | copy-start | bytes 49156
  226.6 15.0 %all-to-all-start.7 = ((f16[8,72,256]{2,1,0:T(8,128)(2,1)}), f16[8,72,256]{2,1,0:T(8,128)(2,1)}, u32[]{:S(2)}, u32[]{:S(2)}) async-start(f16[8,72,256]{2,1,0:T(8,128)(2,1)} %broadcast_in_dim.28), calls=%async_computation.7 | async-start | bytes 589824 | tf_op jit(solution)/shard_map/all_to_all | solution.py:37
  242.6 0.9 copy-start.5
  269.3 22.1 %all-to-all-start.9 = ((f32[64,1,8,128]{3,2,1,0:T(8,128)}), f32[64,1,8,128]{3,2,1,0:T(8,128)S(1)}, u32[]{:S(2)}, u32[]{:S(2)}) async-start(f32[64,1,8,128]{3,2,1,0:T(8,128)} %broadcast_in_dim.29), calls=%async_computation.9 | async-start | bytes 524288 | tf_op jit(solution)/shard_map/all_to_all | solution.py:37
  291.4 0.7 copy-start.9
Sparse Core Ops, SparseCore 0:
  10.1 52.8 all-gather.1

commit v5 on v4

--- a/solution.py
+++ b/solution.py
@@ -186,10 +186,12 @@
     )(core, own, *sketch)
 
 
-def signals_kernel(feed, before, activity, out):
+def signals_kernel(feed, before, marks, activity, out):
     pieces, rows, width = out.shape
     rank = feed.shape[0]
-    prior = product(before[...], feed[...], 1, 1).astype(half)
+    prior = product(before[...], feed[...], 1, 1)
+    upper = lax.broadcasted_iota(jnp.int32, prior.shape, 0) < 8
+    prior = jnp.where(upper, prior, marks[...]).astype(half)
     for i in range(pieces):
         signal = product(feed[...], activity[:, i * width : (i + 1) * width], 1, 0)
         out[i, :rank, :] = signal.astype(half)
@@ -197,20 +199,20 @@
         out[i, rank:, :rank] = prior
 
 
-def signal_parts(feed, before, activity, pieces):
+def signal_parts(feed, before, marks, activity, pieces):
     rank, neurons = feed.shape
     frames = activity.shape[1]
     return pl.pallas_call(
         signals_kernel,
         out_shape=jax.ShapeDtypeStruct((pieces, rank + before.shape[0], frames // pieces), half),
-        in_specs=in_vmem(3),
+        in_specs=in_vmem(4),
         out_specs=in_vmem(1)[0],
         compiler_params=pltpu.CompilerParams(vmem_limit_bytes=16 * 2**20),
         cost_estimate=pl.CostEstimate(
             flops=2 * rank * neurons * frames, bytes_accessed=4 * 2**20, transcendentals=0
         ),
         name="signal_parts",
-    )(feed, before, activity)
+    )(feed, before, marks, activity)
 
 
 def latent_parts(core, gram, sketch, mix, before, activity, pieces):
@@ -413,8 +415,16 @@
     region_feed, spread = region_tables(my_blocks, region_mask, region_in, region_out)
     maps = jnp.concatenate([readout, spread], axis=1)
     rank = region_feed.shape[1]
-    signal = signal_parts(region_feed.T, before, activity, regions)
-    signal = scatter_sum(signal, "region").astype(half)
+    largest = lax.pmax(jnp.max(jnp.abs(test_matrix.astype(full)), axis=0), SLAB)
+    here = jnp.arange(16)[:, None] == 8 + lax.axis_index("region")
+    marks = jnp.where(here, jnp.pad(largest, (0, rank - largest.shape[0]))[None, :], 0.0)
+    signal = signal_parts(region_feed.T, before, marks, activity, regions)
+    signal = scatter_sum(signal, "region")
+    largest = signal[rank + 8 : rank + 8 + regions, : test_matrix.shape[1]].reshape(columns)
+    mid = columns // CORES
+    largest = lax.dynamic_slice_in_dim(jnp.maximum(largest, 1e-30), core * mid, mid)
+    up = (2 / largest).reshape(chips, mid // chips, 1)
+    signal = signal.astype(half)
 
     largest = jnp.maximum(jnp.max(jnp.abs(basis_mix), axis=0), 1e-30)
     width = frames_here // regions
@@ -426,18 +436,20 @@
     )
     unit = unit / 4
     bias = latent_bias[:, None]
-    test_full, signal, maps, before, bias, unit, per_unit = lax.optimization_barrier(
-        (test_full, signal, maps, before, bias, unit, 1 / unit)
-    )
-
-    mid = columns // CORES
+    test_full, signal, maps, before, bias, unit, per_unit, up = lax.optimization_barrier(
+        (test_full, signal, maps, before, bias, unit, 1 / unit, up)
+    )
+
     theirs = product(lax.dynamic_slice_in_dim(test_full, (1 - core) * mid, mid), activity, 1, 1)
     theirs = other_core(theirs)
     mine = product(lax.dynamic_slice_in_dim(test_full, core * mid, mid), activity, 1, 1)
     mine = lax.optimization_barrier(mine) + theirs
-    own = scatter_sum(mine.reshape(chips, mid // chips, neurons_here), "chip")
+    mine = mine.reshape(chips, mid // chips, neurons_here) * up
+    own = scatter_sum(mine.astype(jnp.float16), "chip") / 26
+    own = lax.optimization_barrier(own.astype(jnp.float16))
     mine = share(own, "chip").reshape(mid, neurons_here)
-    sketch = mine, other_core(mine)
+    sketch = mine.astype(full), other_core(mine).astype(full)
+    own = own.astype(full)
 
     core = core.reshape(1)
     rows = lax.all_to_all(gram_rows(core, own, sketch, regions), "region", 0, 0)

time: 302 us -> 383 us (1.27)
  blocking collectives: 148 us -> 256 us
  waiting for transfers between devices: 46.7 us -> 20.3 us
    pmax x0 -> x1, blocking collectives: none -> 114 us  [local(): largest = lax.pmax(jnp.max(jnp.abs(test_matrix.astype(full)), axis=0), SLAB)]
    all_gather x1, waiting for transfers between devices: 16 us -> 0.02 us  [local(): test_full = lax.all_gather(test_matrix.T, 'region', axis=0, tiled=True)]
    all_to_all x2, blocking collectives: 48.8 us -> 39.6 us  [share(): return lax.all_to_all(lax.optimization_barrier(copies), axis, 0, 0)]
    ppermute x1, waiting for transfers between devices: 6.07 us -> 0.01 us  [local(): lax.ppermute(activity[:, -1], SLAB, [(i, i + 1) for i in range(slabs - 1)])]
    all_to_all x3, blocking collectives: 71.1 us -> 75.9 us  [scatter_sum(): return jnp.sum(lax.all_to_all(pieces, axis, 0, 0).astype(full), axis=0)]
    all_to_all x1, waiting for transfers between devices: 8.61 us -> 4.12 us  [scatter_sum(): return jnp.sum(lax.all_to_all(pieces, axis, 0, 0).astype(full), axis=0)]
  transfers between devices with their start and end apart: 9 -> 9, of which waited for: 7 -> 5; matrix products, arithmetic and copies ran while one was open for 5% -> 4% of each run, Pallas kernels for 9% -> 7%
where the time goes in v5:
time: 383 us; the launch traced here: 382 us
  blocking collectives  256 us (67%)
  Pallas kernels  35.3 us (9%)
  starting transfers between devices  28.9 us (8%)
  waiting for transfers between devices  20.3 us (5%)
  between operations  14.4 us (4%)
  local copies, waits for them, and re-layouts  11.5 us (3%)
  other arithmetic  10.5 us (3%)
  matrix products  4.35 us (1%)
    pmax x1, blocking collectives, local(): largest = lax.pmax(jnp.max(jnp.abs(test_matrix.astype(full)), axis=0), SLAB)  114 us
    all_to_all x3, blocking collectives, scatter_sum(): return jnp.sum(lax.all_to_all(pieces, axis, 0, 0).astype(full), axis=0)  75.9 us
    all_to_all x2, blocking collectives, share(): return lax.all_to_all(lax.optimization_barrier(copies), axis, 0, 0)  39.6 us
    pallas_call x1, Pallas kernels, latent_parts(): pl.pallas_call(latents_kernel, out_shape=jax.ShapeDtypeStruct((pieces, ra...  25 us
    psum x1, blocking collectives, local(): frame_sq = lax.psum(frame_sq.reshape(frames_here), 'region')  15 us
    all_to_all x3, starting transfers between devices, share(): return lax.all_to_all(lax.optimization_barrier(copies), axis, 0, 0)  14.1 us
    all_to_all x1, blocking collectives, local(): rows = lax.all_to_all(gram_rows(core, own, sketch, regions), 'region', 0, 0)  12.3 us
    all_to_all x3, waiting for transfers between devices, share(): return lax.all_to_all(lax.optimization_barrier(copies), axis, 0, 0)  10.8 us
  transfers between devices with their start and end apart: 9, of which 5 were waited for; matrix products, arithmetic and copies ran while one was open for 4% of the time, Pallas kernels for 7%

profile of v5, /device:TPU:6, one launch (start us, length us, event | category | flops | bytes accessed | tf_op | source)
XLA Modules:
  0.0 381.7 jit_solution(8254075947066664636)
XLA Ops:
  9.1 1.9 collective-permute-start
  14.2 113.6 %pmax.7 = f32[64]{0:T(128)S(1)} all-reduce(f32[64]{0:T(128)S(1)} %abs_reduce_fusion), channel_id=1, replica_groups=mesh['chip'=32,'core'=2,'region'=8] {'chip','core'}, use_global_device_ids=true, to_apply=%region_1.0 | all-reduce | flops 64 | bytes 512 | tf_op jit(solution)/shard_map/pmax | solution.py:418
  129.7 1.9 copy-done
  132.9 7.1 %all-to-all-start = ((bf16[8,80,256]{2,1,0:T(8,128)(2,1)}), bf16[8,80,256]{2,1,0:T(8,128)(2,1)S(1)}, u32[]{:S(2)}, u32[]{:S(2)}) async-start(bf16[8,80,256]{2,1,0:T(8,128)(2,1)} %signal_parts.1), calls=%async_computation | async-start | bytes 655360 | tf_op jit(solution)/shard_map/all_to_all | solution.py:32
  144.4 1.8 pad_maximum_fusion.maps
  147.0 4.1 %all-to-all-done = bf16[8,80,256]{2,1,0:T(8,128)(2,1)S(1)} async-done(((bf16[8,80,256]{2,1,0:T(8,128)(2,1)}), bf16[8,80,256]{2,1,0:T(8,128)(2,1)S(1)}, u32[]{:S(2)}, u32[]{:S(2)}) %all-to-all-start) | async-done | bytes 327712 | tf_op jit(solution)/shard_map/all_to_all | solution.py:32
  151.5 2.4 fusion
  153.9 1.9 collective-permute-start.1
  158.3 37.3 %all_to_all.50 = f16[32,8,768]{2,1,0:T(8,128)(2,1)S(1)} all-to-all(f16[32,8,768]{2,1,0:T(8,128)(2,1)S(1)} %fusion.4), channel_id=1, replica_groups=mesh['chip'=32,'core'=2,'region'=8] {'chip'}, dimensions={0} | all-to-all | bytes 786432 | tf_op jit(solution)/shard_map/all_to_all | solution.py:32
  195.7 19.2 %all_to_all.51 = f16[32,8,768]{2,1,0:T(8,128)(2,1)S(1)} all-to-all(f16[32,8,768]{2,1,0:T(8,128)(2,1)S(1)} %broadcast_in_dim.48), channel_id=1, replica_groups=mesh['chip'=32,'core'=2,'region'=8] {'chip'}, dimensions={0} | all-to-all | bytes 786432 | tf_op jit(solution)/shard_map/all_to_all | solution.py:37
  214.9 1.9 collective-permute-start.2
  219.9 12.3 %all_to_all.52 = f32[8,8,512]{2,1,0:T(8,128)S(1)} all-to-all(f32[8,8,512]{2,1,0:T(8,128)S(1)} %gram_rows.1), channel_id=1, replica_groups=mesh['chip'=32,'core'=2,'region'=8] {'region'}, dimensions={0} | all-to-all | bytes 262144 | tf_op jit(solution)/shard_map/all_to_all | solution.py:455
  232.3 20.4 %all_to_all.53 = f32[32,8,512]{2,1,0:T(8,128)S(1)} all-to-all(f32[32,8,512]{2,1,0:T(8,128)S(1)} %broadcast_in_dim.49), channel_id=1, replica_groups=mesh['chip'=32,'core'=2,'region'=8] {'chip'}, dimensions={0} | all-to-all | bytes 1048576 | tf_op jit(solution)/shard_map/all_to_all | solution.py:37
  252.7 1.9 collective-permute-start.3
  254.6 1.9 collective-permute-done.3.gram_other
  257.3 3.6 all-to-all-start.5
  260.9 25.0 %latent_parts.1 = f32[8,72,256]{2,1,0:T(8,128)} custom-call(s32[1]{0:T(128)} %bitcast.core, f32[256,512]{1,0:T(8,128)} %bitcast.33, f32[256,512]{1,0:T(8,128)} %copy-done.10, bf16[16,768]{1,0:T(8,128)(2,1)} %copy-done.6, f32[256,768]{1,0:T(8,128)} %copy-done.3, f32[256,768]{1,0:T(8,128)} %copy-done.4, f32[64,512]{1,0:T(8,128)} %bitcast.37, ...), custom_call_target="tpu_custom_call" | custom-call | flops 268435456 | bytes 8388608 | tf_op jit(solution)/shard_map/latent_parts/pallas_call | solution.py:222
  287.3 19.3 %all_to_all.54 = f16[8,72,256]{2,1,0:T(8,128)(2,1)S(1)} all-to-all(f16[8,72,256]{2,1,0:T(8,128)(2,1)S(1)} %multiply_convert_fusion), channel_id=1, replica_groups=mesh['chip'=32,'core'=2,'region'=8] {'region'}, dimensions={0} | all-to-all | bytes 589824 | tf_op jit(solution)/shard_map/all_to_all | solution.py:32
  307.4 4.1 %all-to-all-start.7 = ((f16[8,72,256]{2,1,0:T(8,128)(2,1)}), f16[8,72,256]{2,1,0:T(8,128)(2,1)}, u32[]{:S(2)}, u32[]{:S(2)}) async-start(f16[8,72,256]{2,1,0:T(8,128)(2,1)} %broadcast_in_dim.51), calls=%async_computation.7 | async-start | bytes 589824 | tf_op jit(solution)/shard_map/all_to_all | solution.py:37
  311.6 10.8 %all-to-all-done.7 = f16[8,72,256]{2,1,0:T(8,128)(2,1)} async-done(((f16[8,72,256]{2,1,0:T(8,128)(2,1)}), f16[8,72,256]{2,1,0:T(8,128)(2,1)}, u32[]{:S(2)}, u32[]{:S(2)}) %all-to-all-start.7) | async-done | bytes 294944 | tf_op jit(solution)/shard_map/all_to_all | solution.py:37
  324.4 5.8 %error_stats.1 = (f32[64,2048]{1,0:T(8,128)}, f32[1,2048]{1,0:T(1,128)S(1)}, f32[64,8,128]{2,1,0:T(8,128)S(1)}) custom-call(f32[8,72,256]{2,1,0:T(8,128)S(1)} %convert_multiply_fusion.latents, bf16[8,80,256]{2,1,0:T(8,128)(2,1)S(1)} %all-to-all-done.5.signals, bf16[768,2048]{1,0:T(8,128)(2,1)S(1)} %copy-done.2, bf16[768,128]{1,0:T(8,128)(2,1)S(1)} %copy-done.5, ...), custom_call_target="tpu_custom_call" | custom-call | flops 805306368 | bytes 8388608 | tf_op jit(solution)/shard_map/error_stats/pallas_call | solution.py:323
  330.2 19.2 %all_to_all.55 = f32[64,1,8,128]{3,2,1,0:T(8,128)S(1)} all-to-all(f32[64,1,8,128]{3,2,1,0:T(8,128)S(1)} %bitcast.30), channel_id=1, replica_groups=mesh['chip'=32,'core'=2,'region'=8] {'chip','core'}, dimensions={0} | all-to-all | bytes 524288 | tf_op jit(solution)/shard_map/all_to_all | solution.py:32
  350.2 6.5 %all-to-all-start.9 = ((f32[64,1,8,128]{3,2,1,0:T(8,128)}), f32[64,1,8,128]{3,2,1,0:T(8,128)S(1)}, u32[]{:S(2)}, u32[]{:S(2)}) async-start(f32[64,1,8,128]{3,2,1,0:T(8,128)} %broadcast_in_dim.52), calls=%async_computation.9 | async-start | bytes 524288 | tf_op jit(solution)/shard_map/all_to_all | solution.py:37
  356.7 15.0 %psum.7 = f32[2048]{0:T(1024)S(1)} all-reduce(f32[2048]{0:T(1024)S(1)} %bitcast.31), channel_id=1, replica_groups=mesh['chip'=32,'core'=2,'region'=8] {'region'}, use_global_device_ids=true, to_apply=%region_7.8 | all-reduce | flops 2048 | bytes 16384 | tf_op jit(solution)/shard_map/psum | solution.py:469
  (83 shorter events, 28.3 us)
Async XLA Ops:
  7.2 144.3 %all-gather.2.cloned.1.call-start = ((), (), s32[]{:S(2)}) async-start(), calls=%async_computation.10 | async-start | bytes 2359296 | tf_op jit(solution)/shard_map/all_gather | solution.py:407
  9.1 120.6 %collective-permute-start = (bf16[768]{0:T(1024)(128)(2,1)S(1)}, bf16[768]{0:T(1024)(128)(2,1)S(1)}, u32[]{:S(2)}, u32[]{:S(2)}) collective-permute-start(bf16[768]{0:T(1024)(128)(2,1)S(1)} %slice_reduce_fusion), channel_id=1, source_target_pairs={{0,8},{8,16},{16,24},{24,32},{32,40},{40,48},{48,56},{56,64},{64,7... | collective-permute-start | bytes 4616 | tf_op jit(solution)/shard_map/ppermute | solution.py:408
  129.7 1.9 copy-start
  131.6 19.6 %copy-start.6 = (bf16[16,768]{1,0:T(8,128)(2,1)}, bf16[16,768]{1,0:T(8,128)(2,1)S(1)}, u32[]{:S(2)}) copy-start(bf16[16,768]{1,0:T(8,128)(2,1)S(1)} %broadcast_in_dim.41.before) | copy-start | bytes 73732
  131.6 19.9 %copy-start.1 = (bf16[768,2048]{1,0:T(8,128)(2,1)S(1)}, bf16[768,2048]{1,0:T(8,128)(2,1)}, u32[]{:S(2)}) copy-start(bf16[768,2048]{1,0:T(8,128)(2,1)} %activity.5) | copy-start | bytes 9437188
  132.9 18.3 %all-to-all-start = ((bf16[8,80,256]{2,1,0:T(8,128)(2,1)}), bf16[8,80,256]{2,1,0:T(8,128)(2,1)S(1)}, u32[]{:S(2)}, u32[]{:S(2)}) async-start(bf16[8,80,256]{2,1,0:T(8,128)(2,1)} %signal_parts.1), calls=%async_computation | async-start | bytes 655360 | tf_op jit(solution)/shard_map/all_to_all | solution.py:32
  151.5 4.4 %copy-start.12 = (bf16[512,2048]{1,0:T(8,128)(2,1)S(1)}, bf16[512,2048]{1,0:T(8,128)(2,1)}, u32[]{:S(2)}) copy-start(bf16[512,2048]{1,0:T(8,128)(2,1)} %all-gather.2.cloned.1.call-done) | copy-start | bytes 6291460
  153.9 4.2 %collective-permute-start.1 = (f32[256,768]{1,0:T(8,128)S(1)}, f32[256,768]{1,0:T(8,128)S(1)}, u32[]{:S(2)}, u32[]{:S(2)}) collective-permute-start(f32[256,768]{1,0:T(8,128)S(1)} %fusion), channel_id=1, source_target_pairs={{0,8},{8,0},{1,9},{9,1},{2,10},{10,2},{3,11},{11,3},{4,12},{12,4},... | collective-permute-start | bytes 2359304 | tf_op jit(solution)/shard_map/ppermute | solution.py:28
  214.9 3.6 collective-permute-start.2
  216.9 44.0 %copy-start.3 = (f32[256,768]{1,0:T(8,128)}, f32[256,768]{1,0:T(8,128)S(1)}, u32[]{:S(2)}) copy-start(f32[256,768]{1,0:T(8,128)S(1)} %bitcast_convert_fusion.sketch) | copy-start | bytes 2359300
  218.6 42.3 %copy-start.4 = (f32[256,768]{1,0:T(8,128)}, f32[256,768]{1,0:T(8,128)S(1)}, u32[]{:S(2)}) copy-start(f32[256,768]{1,0:T(8,128)S(1)} %convert_element_type.87.sketch_other) | copy-start | bytes 2359300
  252.7 8.2 %copy-start.8 = (f32[32,8,512]{2,1,0:T(8,128)}, f32[32,8,512]{2,1,0:T(8,128)S(1)}, u32[]{:S(2)}) copy-start(f32[32,8,512]{2,1,0:T(8,128)S(1)} %all_to_all.53) | copy-start | bytes 1572868
  252.7 3.8 collective-permute-start.3
  256.5 4.4 %copy-start.10 = (f32[256,512]{1,0:T(8,128)}, f32[256,512]{1,0:T(8,128)S(1)}, u32[]{:S(2)}) copy-start(f32[256,512]{1,0:T(8,128)S(1)} %collective-permute-done.3.gram_other) | copy-start | bytes 1572868
  257.3 28.7 %all-to-all-start.5 = ((bf16[8,80,256]{2,1,0:T(8,128)(2,1)}), bf16[8,80,256]{2,1,0:T(8,128)(2,1)S(1)}, u32[]{:S(2)}, u32[]{:S(2)}) async-start(bf16[8,80,256]{2,1,0:T(8,128)(2,1)} %broadcast_in_dim.50), calls=%async_computation.5 | async-start | bytes 655360 | tf_op jit(solution)/shard_map/all_to_all | solution.py:37
  260.9 50.6 %copy-start.11 = (f32[64]{0:T(128)S(1)}, f32[64]{0:T(128)}, u32[]{:S(2)}) copy-start(f32[64]{0:T(128)} %param.14) | copy-start | bytes 772
  286.0 37.5 %copy-start.2 = (bf16[768,2048]{1,0:T(8,128)(2,1)S(1)}, bf16[768,2048]{1,0:T(8,128)(2,1)}, u32[]{:S(2)}) copy-start(bf16[768,2048]{1,0:T(8,128)(2,1)} %activity.5) | copy-start | bytes 9437188
  286.0 37.5 %copy-start.7 = (f32[64,64]{1,0:T(8,128)S(1)}, f32[64,64]{1,0:T(8,128)}, u32[]{:S(2)}) copy-start(f32[64,64]{1,0:T(8,128)} %recurrent.1) | copy-start | bytes 49156
  307.4 15.0 %all-to-all-start.7 = ((f16[8,72,256]{2,1,0:T(8,128)(2,1)}), f16[8,72,256]{2,1,0:T(8,128)(2,1)}, u32[]{:S(2)}, u32[]{:S(2)}) async-start(f16[8,72,256]{2,1,0:T(8,128)(2,1)} %broadcast_in_dim.51), calls=%async_computation.7 | async-start | bytes 589824 | tf_op jit(solution)/shard_map/all_to_all | solution.py:37
  323.5 0.9 copy-start.5
  350.2 22.1 %all-to-all-start.9 = ((f32[64,1,8,128]{3,2,1,0:T(8,128)}), f32[64,1,8,128]{3,2,1,0:T(8,128)S(1)}, u32[]{:S(2)}, u32[]{:S(2)}) async-start(f32[64,1,8,128]{3,2,1,0:T(8,128)} %broadcast_in_dim.52), calls=%async_computation.9 | async-start | bytes 524288 | tf_op jit(solution)/shard_map/all_to_all | solution.py:37
  372.3 0.7 copy-start.9
Sparse Core Ops, SparseCore 0:
  10.1 48.1 all-gather.1

commit v6 on v5

--- a/solution.py
+++ b/solution.py
@@ -415,7 +415,10 @@
     region_feed, spread = region_tables(my_blocks, region_mask, region_in, region_out)
     maps = jnp.concatenate([readout, spread], axis=1)
     rank = region_feed.shape[1]
-    largest = lax.pmax(jnp.max(jnp.abs(test_matrix.astype(full)), axis=0), SLAB)
+    largest = jnp.max(jnp.abs(test_matrix.astype(full)), axis=0)
+    block = jnp.pad(largest, (0, BLOCK - largest.shape[0]))
+    block = jnp.max(share(jnp.broadcast_to(block[None], (8, BLOCK)), SLAB), axis=0)
+    largest = block[0, : largest.shape[0]]
     here = jnp.arange(16)[:, None] == 8 + lax.axis_index("region")
     marks = jnp.where(here, jnp.pad(largest, (0, rank - largest.shape[0]))[None, :], 0.0)
     signal = signal_parts(region_feed.T, before, marks, activity, regions)

time: 383 us -> 283 us (0.74)
  blocking collectives: 256 us -> 131 us
  starting transfers between devices: 28.9 us -> 43.1 us
  waiting for transfers between devices: 20.3 us -> 31.2 us
    pmax x1 -> x0, blocking collectives: 114 us -> none  [local(): largest = lax.pmax(jnp.max(jnp.abs(test_matrix.astype(full)), axis=0), SLAB)]
    all_to_all x3 -> x4, starting transfers between devices: 14.1 us -> 28.2 us  [share(): return lax.all_to_all(lax.optimization_barrier(copies), axis, 0, 0)]
    all_to_all x3, blocking collectives: 75.9 us -> 62.5 us  [scatter_sum(): return jnp.sum(lax.all_to_all(pieces, axis, 0, 0).astype(full), axis=0)]
    all_to_all x1, waiting for transfers between devices: 4.12 us -> 10 us  [scatter_sum(): return jnp.sum(lax.all_to_all(pieces, axis, 0, 0).astype(full), axis=0)]
    all_to_all x3 -> x4, waiting for transfers between devices: 10.8 us -> 15.3 us  [share(): return lax.all_to_all(lax.optimization_barrier(copies), axis, 0, 0)]
  transfers between devices with their start and end apart: 9 -> 10, of which waited for: 5 -> 7; matrix products, arithmetic and copies ran while one was open for 4% -> 6% of each run, Pallas kernels for 7% -> 9%
where the time goes in v6:
time: 283 us; the launch traced here: 282 us
  blocking collectives  131 us (46%)
  starting transfers between devices  43.1 us (15%)
  Pallas kernels  35.3 us (12%)
  waiting for transfers between devices  31.2 us (11%)
  between operations  14.4 us (5%)
  local copies, waits for them, and re-layouts  12.2 us (4%)
  other arithmetic  10.5 us (4%)
  matrix products  4.34 us (2%)
    all_to_all x3, blocking collectives, scatter_sum(): return jnp.sum(lax.all_to_all(pieces, axis, 0, 0).astype(full), axis=0)  62.5 us
    all_to_all x2, blocking collectives, share(): return lax.all_to_all(lax.optimization_barrier(copies), axis, 0, 0)  39.4 us
    all_to_all x4, starting transfers between devices, share(): return lax.all_to_all(lax.optimization_barrier(copies), axis, 0, 0)  28.2 us
    pallas_call x1, Pallas kernels, latent_parts(): pl.pallas_call(latents_kernel, out_shape=jax.ShapeDtypeStruct((pieces, ra...  25.1 us
    all_to_all x4, waiting for transfers between devices, share(): return lax.all_to_all(lax.optimization_barrier(copies), axis, 0, 0)  15.3 us
    psum x1, blocking collectives, local(): frame_sq = lax.psum(frame_sq.reshape(frames_here), 'region')  15 us
    all_to_all x1, blocking collectives, local(): rows = lax.all_to_all(gram_rows(core, own, sketch, regions), 'region', 0, 0)  13.7 us
    all_to_all x1, waiting for transfers between devices, scatter_sum(): return jnp.sum(lax.all_to_all(pieces, axis, 0, 0).astype(full), axis=0)  10 us
  transfers between devices with their start and end apart: 10, of which 7 were waited for; matrix products, arithmetic and copies ran while one was open for 6% of the time, Pallas kernels for 9%

profile of v6, /device:TPU:6, one launch (start us, length us, event | category | flops | bytes accessed | tf_op | source)
XLA Modules:
  0.0 281.9 jit_solution(7768720617944031023)
XLA Ops:
  9.7 14.0 %all-to-all-start = ((f32[64,8,128]{2,1,0:T(8,128)}), f32[64,8,128]{2,1,0:T(8,128)S(1)}, u32[]{:S(2)}, u32[]{:S(2)}) async-start(f32[64,8,128]{2,1,0:T(8,128)} %broadcast_in_dim_broadcast_in_dim_broadcast_in_dim.2), calls=%async_computation | async-start | bytes 524288 | tf_op jit(solution)/shard_map/all_to_all | solution.py:37
  24.9 2.1 collective-permute-start
  30.9 4.4 %all-to-all-done = f32[64,8,128]{2,1,0:T(8,128)S(1)} async-done(((f32[64,8,128]{2,1,0:T(8,128)}), f32[64,8,128]{2,1,0:T(8,128)S(1)}, u32[]{:S(2)}, u32[]{:S(2)}) %all-to-all-start) | async-done | bytes 262176 | tf_op jit(solution)/shard_map/all_to_all | solution.py:37
  35.5 1.9 copy-done
  38.7 7.1 %all-to-all-start.1 = ((bf16[8,80,256]{2,1,0:T(8,128)(2,1)}), bf16[8,80,256]{2,1,0:T(8,128)(2,1)S(1)}, u32[]{:S(2)}, u32[]{:S(2)}) async-start(bf16[8,80,256]{2,1,0:T(8,128)(2,1)} %signal_parts.1), calls=%async_computation.1 | async-start | bytes 655360 | tf_op jit(solution)/shard_map/all_to_all | solution.py:32
  52.9 10.0 %all-to-all-done.1 = bf16[8,80,256]{2,1,0:T(8,128)(2,1)S(1)} async-done(((bf16[8,80,256]{2,1,0:T(8,128)(2,1)}), bf16[8,80,256]{2,1,0:T(8,128)(2,1)S(1)}, u32[]{:S(2)}, u32[]{:S(2)}) %all-to-all-start.1) | async-done | bytes 327712 | tf_op jit(solution)/shard_map/all_to_all | solution.py:32
  63.8 2.4 fusion
  66.2 1.9 collective-permute-start.1
  70.5 23.9 %all_to_all.55 = f16[32,8,768]{2,1,0:T(8,128)(2,1)S(1)} all-to-all(f16[32,8,768]{2,1,0:T(8,128)(2,1)S(1)} %fusion.4), channel_id=1, replica_groups=mesh['chip'=32,'core'=2,'region'=8] {'chip'}, dimensions={0} | all-to-all | bytes 786432 | tf_op jit(solution)/shard_map/all_to_all | solution.py:32
  94.6 19.0 %all_to_all.56 = f16[32,8,768]{2,1,0:T(8,128)(2,1)S(1)} all-to-all(f16[32,8,768]{2,1,0:T(8,128)(2,1)S(1)} %broadcast_in_dim.51), channel_id=1, replica_groups=mesh['chip'=32,'core'=2,'region'=8] {'chip'}, dimensions={0} | all-to-all | bytes 786432 | tf_op jit(solution)/shard_map/all_to_all | solution.py:37
  113.6 1.9 collective-permute-start.2
  118.6 13.7 %all_to_all.57 = f32[8,8,512]{2,1,0:T(8,128)S(1)} all-to-all(f32[8,8,512]{2,1,0:T(8,128)S(1)} %gram_rows.1), channel_id=1, replica_groups=mesh['chip'=32,'core'=2,'region'=8] {'region'}, dimensions={0} | all-to-all | bytes 262144 | tf_op jit(solution)/shard_map/all_to_all | solution.py:458
  132.5 20.4 %all_to_all.58 = f32[32,8,512]{2,1,0:T(8,128)S(1)} all-to-all(f32[32,8,512]{2,1,0:T(8,128)S(1)} %broadcast_in_dim.52), channel_id=1, replica_groups=mesh['chip'=32,'core'=2,'region'=8] {'chip'}, dimensions={0} | all-to-all | bytes 1048576 | tf_op jit(solution)/shard_map/all_to_all | solution.py:37
  152.9 1.9 collective-permute-start.3
  154.8 1.9 collective-permute-done.3.gram_other
  157.5 3.6 %all-to-all-start.6 = ((bf16[8,80,256]{2,1,0:T(8,128)(2,1)}), bf16[8,80,256]{2,1,0:T(8,128)(2,1)S(1)}, u32[]{:S(2)}, u32[]{:S(2)}) async-start(bf16[8,80,256]{2,1,0:T(8,128)(2,1)} %broadcast_in_dim.53), calls=%async_computation.6 | async-start | bytes 655360 | tf_op jit(solution)/shard_map/all_to_all | solution.py:37
  161.1 25.1 %latent_parts.1 = f32[8,72,256]{2,1,0:T(8,128)} custom-call(s32[1]{0:T(128)} %bitcast.core, f32[256,512]{1,0:T(8,128)} %bitcast.35, f32[256,512]{1,0:T(8,128)} %copy-done.10, bf16[16,768]{1,0:T(8,128)(2,1)} %copy-done.6, f32[256,768]{1,0:T(8,128)} %copy-done.3, f32[256,768]{1,0:T(8,128)} %copy-done.4, f32[64,512]{1,0:T(8,128)} %bitcast.39, ...), custom_call_target="tpu_custom_call" | custom-call | flops 268435456 | bytes 8388608 | tf_op jit(solution)/shard_map/latent_parts/pallas_call | solution.py:222
  187.5 19.3 %all_to_all.59 = f16[8,72,256]{2,1,0:T(8,128)(2,1)S(1)} all-to-all(f16[8,72,256]{2,1,0:T(8,128)(2,1)S(1)} %multiply_convert_fusion), channel_id=1, replica_groups=mesh['chip'=32,'core'=2,'region'=8] {'region'}, dimensions={0} | all-to-all | bytes 589824 | tf_op jit(solution)/shard_map/all_to_all | solution.py:32
  207.6 4.1 %all-to-all-start.8 = ((f16[8,72,256]{2,1,0:T(8,128)(2,1)}), f16[8,72,256]{2,1,0:T(8,128)(2,1)}, u32[]{:S(2)}, u32[]{:S(2)}) async-start(f16[8,72,256]{2,1,0:T(8,128)(2,1)} %broadcast_in_dim.54), calls=%async_computation.8 | async-start | bytes 589824 | tf_op jit(solution)/shard_map/all_to_all | solution.py:37
  211.8 10.8 %all-to-all-done.8 = f16[8,72,256]{2,1,0:T(8,128)(2,1)} async-done(((f16[8,72,256]{2,1,0:T(8,128)(2,1)}), f16[8,72,256]{2,1,0:T(8,128)(2,1)}, u32[]{:S(2)}, u32[]{:S(2)}) %all-to-all-start.8) | async-done | bytes 294944 | tf_op jit(solution)/shard_map/all_to_all | solution.py:37
  224.6 5.8 %error_stats.1 = (f32[64,2048]{1,0:T(8,128)}, f32[1,2048]{1,0:T(1,128)S(1)}, f32[64,8,128]{2,1,0:T(8,128)S(1)}) custom-call(f32[8,72,256]{2,1,0:T(8,128)S(1)} %convert_multiply_fusion.latents, bf16[8,80,256]{2,1,0:T(8,128)(2,1)S(1)} %all-to-all-done.6.signals, bf16[768,2048]{1,0:T(8,128)(2,1)S(1)} %copy-done.2, bf16[768,128]{1,0:T(8,128)(2,1)S(1)} %copy-done.5, ...), custom_call_target="tpu_custom_call" | custom-call | flops 805306368 | bytes 8388608 | tf_op jit(solution)/shard_map/error_stats/pallas_call | solution.py:323
  230.4 19.2 %all_to_all.60 = f32[64,1,8,128]{3,2,1,0:T(8,128)S(1)} all-to-all(f32[64,1,8,128]{3,2,1,0:T(8,128)S(1)} %bitcast.32), channel_id=1, replica_groups=mesh['chip'=32,'core'=2,'region'=8] {'chip','core'}, dimensions={0} | all-to-all | bytes 524288 | tf_op jit(solution)/shard_map/all_to_all | solution.py:32
  250.4 6.5 %all-to-all-start.10 = ((f32[64,1,8,128]{3,2,1,0:T(8,128)}), f32[64,1,8,128]{3,2,1,0:T(8,128)S(1)}, u32[]{:S(2)}, u32[]{:S(2)}) async-start(f32[64,1,8,128]{3,2,1,0:T(8,128)} %broadcast_in_dim.55), calls=%async_computation.10 | async-start | bytes 524288 | tf_op jit(solution)/shard_map/all_to_all | solution.py:37
  256.9 15.0 %psum.7 = f32[2048]{0:T(1024)S(1)} all-reduce(f32[2048]{0:T(1024)S(1)} %bitcast.33), channel_id=1, replica_groups=mesh['chip'=32,'core'=2,'region'=8] {'region'}, use_global_device_ids=true, to_apply=%region_7.8 | all-reduce | flops 2048 | bytes 16384 | tf_op jit(solution)/shard_map/psum | solution.py:472
  (88 shorter events, 31.4 us)
Async XLA Ops:
  7.2 56.6 %all-gather.2.cloned.1.call-start = ((), (), s32[]{:S(2)}) async-start(), calls=%async_computation.11 | async-start | bytes 2359296 | tf_op jit(solution)/shard_map/all_gather | solution.py:407
  9.7 25.6 %all-to-all-start = ((f32[64,8,128]{2,1,0:T(8,128)}), f32[64,8,128]{2,1,0:T(8,128)S(1)}, u32[]{:S(2)}, u32[]{:S(2)}) async-start(f32[64,8,128]{2,1,0:T(8,128)} %broadcast_in_dim_broadcast_in_dim_broadcast_in_dim.2), calls=%async_computation | async-start | bytes 524288 | tf_op jit(solution)/shard_map/all_to_all | solution.py:37
  24.9 10.6 %collective-permute-start = (bf16[768]{0:T(1024)(128)(2,1)S(1)}, bf16[768]{0:T(1024)(128)(2,1)S(1)}, u32[]{:S(2)}, u32[]{:S(2)}) collective-permute-start(bf16[768]{0:T(1024)(128)(2,1)S(1)} %slice_reduce_fusion), channel_id=1, source_target_pairs={{0,8},{8,16},{16,24},{24,32},{32,40},{40,48},{48,56},{56,64},{64,7... | collective-permute-start | bytes 4616 | tf_op jit(solution)/shard_map/ppermute | solution.py:408
  35.5 1.9 copy-start
  37.4 25.5 %copy-start.6 = (bf16[16,768]{1,0:T(8,128)(2,1)}, bf16[16,768]{1,0:T(8,128)(2,1)S(1)}, u32[]{:S(2)}) copy-start(bf16[16,768]{1,0:T(8,128)(2,1)S(1)} %broadcast_in_dim.43.before) | copy-start | bytes 73732
  37.4 26.4 %copy-start.1 = (bf16[768,2048]{1,0:T(8,128)(2,1)S(1)}, bf16[768,2048]{1,0:T(8,128)(2,1)}, u32[]{:S(2)}) copy-start(bf16[768,2048]{1,0:T(8,128)(2,1)} %activity.5) | copy-start | bytes 9437188
  38.7 24.2 %all-to-all-start.1 = ((bf16[8,80,256]{2,1,0:T(8,128)(2,1)}), bf16[8,80,256]{2,1,0:T(8,128)(2,1)S(1)}, u32[]{:S(2)}, u32[]{:S(2)}) async-start(bf16[8,80,256]{2,1,0:T(8,128)(2,1)} %signal_parts.1), calls=%async_computation.1 | async-start | bytes 655360 | tf_op jit(solution)/shard_map/all_to_all | solution.py:32
  63.8 4.3 %copy-start.12 = (bf16[512,2048]{1,0:T(8,128)(2,1)S(1)}, bf16[512,2048]{1,0:T(8,128)(2,1)}, u32[]{:S(2)}) copy-start(bf16[512,2048]{1,0:T(8,128)(2,1)} %all-gather.2.cloned.1.call-done) | copy-start | bytes 6291460
  66.2 4.2 %collective-permute-start.1 = (f32[256,768]{1,0:T(8,128)S(1)}, f32[256,768]{1,0:T(8,128)S(1)}, u32[]{:S(2)}, u32[]{:S(2)}) collective-permute-start(f32[256,768]{1,0:T(8,128)S(1)} %fusion), channel_id=1, source_target_pairs={{0,8},{8,0},{1,9},{9,1},{2,10},{10,2},{3,11},{11,3},{4,12},{12,4},... | collective-permute-start | bytes 2359304 | tf_op jit(solution)/shard_map/ppermute | solution.py:28
  113.6 3.6 %collective-permute-start.2 = (f16[256,768]{1,0:T(8,128)(2,1)S(1)}, f16[256,768]{1,0:T(8,128)(2,1)S(1)}, u32[]{:S(2)}, u32[]{:S(2)}) collective-permute-start(f16[256,768]{1,0:T(8,128)(2,1)S(1)} %bitcast.36), channel_id=1, source_target_pairs={{0,8},{8,0},{1,9},{9,1},{2,10},{10,2},{3,11},{11,3},{4,12},{12,4},... | collective-permute-start | bytes 1179656 | tf_op jit(solution)/shard_map/ppermute | solution.py:28
  115.6 45.5 %copy-start.3 = (f32[256,768]{1,0:T(8,128)}, f32[256,768]{1,0:T(8,128)S(1)}, u32[]{:S(2)}) copy-start(f32[256,768]{1,0:T(8,128)S(1)} %bitcast_convert_fusion.sketch) | copy-start | bytes 2359300
  117.3 43.8 %copy-start.4 = (f32[256,768]{1,0:T(8,128)}, f32[256,768]{1,0:T(8,128)S(1)}, u32[]{:S(2)}) copy-start(f32[256,768]{1,0:T(8,128)S(1)} %convert_element_type.89.sketch_other) | copy-start | bytes 2359300
  152.9 8.2 %copy-start.8 = (f32[32,8,512]{2,1,0:T(8,128)}, f32[32,8,512]{2,1,0:T(8,128)S(1)}, u32[]{:S(2)}) copy-start(f32[32,8,512]{2,1,0:T(8,128)S(1)} %all_to_all.58) | copy-start | bytes 1572868
  152.9 3.8 %collective-permute-start.3 = (f32[256,512]{1,0:T(8,128)S(1)}, f32[256,512]{1,0:T(8,128)S(1)}, u32[]{:S(2)}, u32[]{:S(2)}) collective-permute-start(f32[256,512]{1,0:T(8,128)S(1)} %bitcast.34), channel_id=1, source_target_pairs={{0,8},{8,0},{1,9},{9,1},{2,10},{10,2},{3,11},{11,3},{4,12},{12,4},... | collective-permute-start | bytes 1572872 | tf_op jit(solution)/shard_map/ppermute | solution.py:28
  156.7 4.4 %copy-start.10 = (f32[256,512]{1,0:T(8,128)}, f32[256,512]{1,0:T(8,128)S(1)}, u32[]{:S(2)}) copy-start(f32[256,512]{1,0:T(8,128)S(1)} %collective-permute-done.3.gram_other) | copy-start | bytes 1572868
  157.5 28.8 %all-to-all-start.6 = ((bf16[8,80,256]{2,1,0:T(8,128)(2,1)}), bf16[8,80,256]{2,1,0:T(8,128)(2,1)S(1)}, u32[]{:S(2)}, u32[]{:S(2)}) async-start(bf16[8,80,256]{2,1,0:T(8,128)(2,1)} %broadcast_in_dim.53), calls=%async_computation.6 | async-start | bytes 655360 | tf_op jit(solution)/shard_map/all_to_all | solution.py:37
  161.1 50.6 %copy-start.11 = (f32[64]{0:T(128)S(1)}, f32[64]{0:T(128)}, u32[]{:S(2)}) copy-start(f32[64]{0:T(128)} %param.14) | copy-start | bytes 772
  186.2 37.5 %copy-start.2 = (bf16[768,2048]{1,0:T(8,128)(2,1)S(1)}, bf16[768,2048]{1,0:T(8,128)(2,1)}, u32[]{:S(2)}) copy-start(bf16[768,2048]{1,0:T(8,128)(2,1)} %activity.5) | copy-start | bytes 9437188
  186.2 37.5 %copy-start.7 = (f32[64,64]{1,0:T(8,128)S(1)}, f32[64,64]{1,0:T(8,128)}, u32[]{:S(2)}) copy-start(f32[64,64]{1,0:T(8,128)} %recurrent.1) | copy-start | bytes 49156
  207.6 15.0 %all-to-all-start.8 = ((f16[8,72,256]{2,1,0:T(8,128)(2,1)}), f16[8,72,256]{2,1,0:T(8,128)(2,1)}, u32[]{:S(2)}, u32[]{:S(2)}) async-start(f16[8,72,256]{2,1,0:T(8,128)(2,1)} %broadcast_in_dim.54), calls=%async_computation.8 | async-start | bytes 589824 | tf_op jit(solution)/shard_map/all_to_all | solution.py:37
  223.7 0.9 copy-start.5
  250.4 22.1 %all-to-all-start.10 = ((f32[64,1,8,128]{3,2,1,0:T(8,128)}), f32[64,1,8,128]{3,2,1,0:T(8,128)S(1)}, u32[]{:S(2)}, u32[]{:S(2)}) async-start(f32[64,1,8,128]{3,2,1,0:T(8,128)} %broadcast_in_dim.55), calls=%async_computation.10 | async-start | bytes 524288 | tf_op jit(solution)/shard_map/all_to_all | solution.py:37
  272.5 0.7 copy-start.9
Sparse Core Ops, SparseCore 0:
  10.1 53.6 all-gather.1
